TPU v7x, 32 devices: a whole 2x2x4 slice. The times are simulated.
32 devices in a mesh: dp: 8 (over z, y), mp: 4 (over x, core).
Axes of the slice: x: 2, y: 2, z: 4, core: 2. Of those that a mesh axis runs over, the one named last changes fastest.
Arguments:
- patches: bfloat16 [16, 64, 32, 512], P('mp', 'dp'), may hold values from -6 to 6
- cotangent: float32 [16, 64, 32, 512], P('mp', 'dp'), may hold values from -40 to 40
- grid_shape: int32 [64, 2], P('dp'), may hold values from 8 to 32, as said below
- qkv_weight: float32 [512, 3, 512], P('dp', None, 'mp'), may hold values from -0.25 to 0.25
- qkv_mean: float32 [512, 3, 512], P('dp', None, 'mp'), may hold values from -0.0009765625 to 0.0009765625
- qkv_square: float32 [512, 3, 512], P('dp', None, 'mp'), may hold values from 3.142093e-10 to 1.2568372e-09
- proj_weight: float32 [512, 512], P('dp', 'mp'), may hold values from -0.25 to 0.25
- proj_mean: float32 [512, 512], P('dp', 'mp'), may hold values from -0.0009765625 to 0.0009765625
- proj_square: float32 [512, 512], P('dp', 'mp'), may hold values from 3.142093e-10 to 1.2568372e-09
- expand_weight: float32 [512, 2048], P('dp', 'mp'), may hold values from -3 to 3
- expand_mean: float32 [512, 2048], P('dp', 'mp'), may hold values from -0.0004272461 to 0.0004272461
- expand_square: float32 [512, 2048], P('dp', 'mp'), may hold values from 7.8552324e-11 to 3.142093e-10
- contract_weight: float32 [512, 2048], P('dp', 'mp'), may hold values from -0.125 to 0.125
- contract_mean: float32 [512, 2048], P('dp', 'mp'), may hold values from -0.0009765625 to 0.0009765625
- contract_square: float32 [512, 2048], P('dp', 'mp'), may hold values from 3.142093e-10 to 1.2568372e-09
- small_params: float32 [72, 512], replicated, may hold values from -4 to 7
- small_mean: float32 [72, 512], replicated, may hold values from -0.0029296875 to 0.0029296875
- small_square: float32 [72, 512], replicated, may hold values from 2.8278837e-09 to 1.1311535e-08
Outputs:
- block_out: bfloat16 [16, 64, 32, 512], P('mp', 'dp')
- patch_grad: float32 [16, 64, 32, 512], P('mp', 'dp')
- grad_norm: float32 [], replicated
- qkv_updated: float32 [512, 3, 512], P('dp', None, 'mp')
- qkv_moment: float32 [512, 3, 512], P('dp', None, 'mp')
- qkv_variance: float32 [512, 3, 512], P('dp', None, 'mp')
- proj_updated: float32 [512, 512], P('dp', 'mp')
- proj_moment: float32 [512, 512], P('dp', 'mp')
- proj_variance: float32 [512, 512], P('dp', 'mp')
- expand_updated: float32 [512, 2048], P('dp', 'mp')
- expand_moment: float32 [512, 2048], P('dp', 'mp')
- expand_variance: float32 [512, 2048], P('dp', 'mp')
- contract_updated: float32 [512, 2048], P('dp', 'mp')
- contract_moment: float32 [512, 2048], P('dp', 'mp')
- contract_variance: float32 [512, 2048], P('dp', 'mp')
- small_updated: float32 [72, 512], replicated
- small_moment: float32 [72, 512], replicated
- small_variance: float32 [72, 512], replicated
Inputs may be any that keep to these rules, and one draw needn't show every extreme that they name: `grid_shape`: row i holds the height and width of image i's patch grid, placed at the canvas's top left; every aligned block of 8 images holds one image that fills the whole 16 x 32 canvas.
All inputs are finite; a program needn't handle non-finite values.
Results may differ from a plain program's by a relative error of at most 0.022.
Values may be sent and summed in bfloat16 or wider, within the bound.
No kernel may reach another device: no remote copies, remote signals or barrier semaphores. Data moves between devices by JAX's collectives and lax.ppermute only.
A program may use at most 192 MiB of HBM per device.

v0:
```python
import math

import jax
import jax.numpy as jnp
from jax import lax
from jax.sharding import PartitionSpec as P

D = 512
HD = 64
FF = 2048
STEP = 10


NORM_EPS = 1e-06
CLIP_NORM = 1.0
BETA_ONE = 0.9
BETA_TWO = 0.999
ADAM_EPS = 1e-08
WEIGHT_DECAY = 0.05
RATE_FACTOR = 2.0
SMALL_RATE = 0.5
ROOT_HALF = 0.7071067811865476
INV_ROOT_TAU = 0.3989422804014327


def extended(cells, sides, width):
    for axis, dim in sides:
        count = lax.axis_size(axis)
        ends = count - 1
        head = lax.slice_in_dim(cells, 0, width, axis=dim)
        tail = lax.slice_in_dim(cells, cells.shape[dim] - width, cells.shape[dim], axis=dim)
        cells = jnp.concatenate(
            [
                lax.ppermute(tail, axis, [(i, (i + 1) % count) for i in range(ends)]),
                cells,
                lax.ppermute(head, axis, [((i + 1) % count, i) for i in range(ends)]),
            ],
            axis=dim,
        )
    return cells


def split_up(array, dim, size):
    before, after = (array.shape[:dim], array.shape[dim + 1 :])
    return jnp.moveaxis(array.reshape(*before, size, -1, *after), dim, 0)


def sent_and_summed(array, axis, dim):
    size = lax.axis_size(axis)
    tiles = lax.all_to_all(split_up(array, dim, size), axis, 0, 0, tiled=True)
    return jnp.sum(tiles.astype(jnp.float32), axis=0)


def side_by_side(arrays, axis, dim, along):
    widths = [math.prod(a.shape[along:]) for a in arrays]
    both = jnp.concatenate(
        [a.reshape(*a.shape[:along], w) for a, w in zip(arrays, widths)], axis=along
    )
    whole = sent_and_summed(both, axis, dim)
    tiles = jnp.split(whole, [sum(widths[:k]) for k in range(1, len(widths))], axis=along)
    return tuple((b.reshape(*whole.shape[:along], *a.shape[along:]) for a, b in zip(arrays, tiles)))


def canvas_mask(grid_shape, first_row, row_count, col_count):
    row_index = first_row + jnp.arange(row_count, dtype=jnp.int32)
    col_index = jnp.arange(col_count, dtype=jnp.int32)
    inside_rows = row_index[:, None, None] < grid_shape[:, 0][None, :, None]
    inside_cols = col_index[None, None, :] < grid_shape[:, 1][None, :, None]
    return (inside_rows & inside_cols).astype(jnp.float32)


def window_mask(first_chan, chan_count):
    head_index = (first_chan + jnp.arange(chan_count, dtype=jnp.int32)) // HD
    radius = jnp.where(head_index < 2, 1, jnp.where(head_index < 5, 2, 3))
    tap_list = jnp.arange(49, dtype=jnp.int32)
    tap_row = jnp.abs(tap_list // 7 - 3)
    tap_col = jnp.abs(tap_list % 7 - 3)
    inside = (tap_row[:, None] <= radius[None, :]) & (tap_col[:, None] <= radius[None, :])
    return inside.astype(jnp.float32)


def depthwise(padded, kernel, reach_cells):
    tap_side = 2 * reach_cells + 1
    row_count = padded.shape[0] - 2 * reach_cells
    col_count = padded.shape[2] - 2 * reach_cells
    result = None
    for tap_index in range(tap_side * tap_side):
        tap_row = tap_index // tap_side
        tap_col = tap_index % tap_side
        term = (
            kernel[tap_index]
            * padded[tap_row : tap_row + row_count, :, tap_col : tap_col + col_count, :]
        )
        result = term if result is None else result + term
    return result


def transposed(padded, kernel, reach_cells):
    tap_side = 2 * reach_cells + 1
    row_count = padded.shape[0] - 2 * reach_cells
    col_count = padded.shape[2] - 2 * reach_cells
    result = None
    for tap_index in range(tap_side * tap_side):
        tap_row = tap_side - 1 - tap_index // tap_side
        tap_col = tap_side - 1 - tap_index % tap_side
        term = (
            kernel[tap_index]
            * padded[tap_row : tap_row + row_count, :, tap_col : tap_col + col_count, :]
        )
        result = term if result is None else result + term
    return result


def tap_sums(padded, gradient, reach_cells):
    tap_side = 2 * reach_cells + 1
    row_count = gradient.shape[0]
    col_count = gradient.shape[2]
    sums_list = []
    for tap_index in range(tap_side * tap_side):
        tap_row = tap_index // tap_side
        tap_col = tap_index % tap_side
        window = padded[tap_row : tap_row + row_count, :, tap_col : tap_col + col_count, :]
        sums_list.append(jnp.sum(gradient * window, axis=(0, 1, 2)))
    return jnp.stack(sums_list)


def cell_sums(values):
    return jnp.sum(values, axis=(0, 1, 2))


def norm_parts(values):
    center = values - jnp.mean(values, axis=-1, keepdims=True)
    rstd = lax.rsqrt(jnp.mean(center * center, axis=-1, keepdims=True) + NORM_EPS)
    return (center * rstd, rstd)


def norm_back(gradient, normed, rstd, gain_row):
    scaled = gradient * gain_row
    return rstd * (
        scaled
        - jnp.mean(scaled, axis=-1, keepdims=True)
        - normed * jnp.mean(scaled * normed, axis=-1, keepdims=True)
    )


def gelu_slope(values):
    normal_cdf = 0.5 * (1.0 + lax.erf(values * ROOT_HALF))
    return normal_cdf + values * jnp.exp(-0.5 * values * values) * INV_ROOT_TAU


def adamw(weight, mean, square, gradient, factor, rate, decay):
    clipped = gradient * factor
    mean_new = BETA_ONE * mean + (1.0 - BETA_ONE) * clipped
    square_new = BETA_TWO * square + (1.0 - BETA_TWO) * clipped * clipped
    mean_hat = mean_new / (1.0 - BETA_ONE**STEP)
    square_hat = square_new / (1.0 - BETA_TWO**STEP)
    weight_new = weight - rate * (mean_hat / (jnp.sqrt(square_hat) + ADAM_EPS) + decay * weight)
    return (weight_new, mean_new, square_new)


def on_device(
    patches,
    cotangent,
    grid_shape,
    qkv_weight,
    qkv_mean,
    qkv_square,
    proj_weight,
    proj_mean,
    proj_square,
    expand_weight,
    expand_mean,
    expand_square,
    contract_weight,
    contract_mean,
    contract_square,
    small_params,
    small_mean,
    small_square,
):
    local_rows, image_count, col_count, channels = patches.shape
    group_size = lax.axis_size("mp")
    position = lax.axis_index("mp")
    all_rows = local_rows * group_size
    head_width = qkv_weight.shape[2]
    hidden_width = expand_weight.shape[1]
    heads_here = head_width // HD
    first_chan = position * head_width
    first_unit = position * hidden_width
    unit_bias_all = small_params[68:].reshape(-1)
    query_bias = lax.dynamic_slice_in_dim(small_params[61], first_chan, head_width)
    value_bias = lax.dynamic_slice_in_dim(small_params[62], first_chan, head_width)
    near_bias = lax.dynamic_slice_in_dim(small_params[63], first_chan, head_width)
    window = window_mask(first_chan, head_width)
    near_kern = lax.dynamic_slice_in_dim(small_params[9:58], first_chan, head_width, 1) * window
    cpe_kern = small_params[0:9]
    qkv_all, proj_all, expand_all, contract_all = (
        lax.all_gather(qkv_weight.astype(jnp.bfloat16), "dp", axis=0, tiled=True),
        lax.all_gather(proj_weight.astype(jnp.bfloat16), "dp", axis=0, tiled=True),
        lax.all_gather(expand_weight.astype(jnp.bfloat16), "dp", axis=0, tiled=True),
        lax.all_gather(contract_weight.astype(jnp.bfloat16), "dp", axis=0, tiled=True),
    )
    own_keep = canvas_mask(grid_shape, position * local_rows, local_rows, col_count)[..., None]
    keep_all = canvas_mask(grid_shape, 0, all_rows, col_count)[..., None]
    masked_in = patches * own_keep.astype(jnp.bfloat16)
    in_edges = extended(masked_in, (("mp", 0),), 1)
    in_pad = jnp.pad(in_edges.astype(jnp.float32), ((0, 0), (0, 0), (1, 1), (0, 0)))
    first_sum = masked_in.astype(jnp.float32) + depthwise(in_pad, cpe_kern, 1) + small_params[58]
    normed_one, rstd_one = norm_parts(first_sum)
    attn_in = (normed_one * small_params[59] + small_params[60]).astype(jnp.bfloat16)
    attn_all = lax.all_gather(attn_in, "mp", axis=0, tiled=True)
    projected = jnp.einsum("yixd,dke->yixke", attn_all, qkv_all, preferred_element_type=jnp.float32)
    query = (projected[..., 0, :] + query_bias).astype(jnp.bfloat16)
    key_raw = projected[..., 1, :]
    value = (projected[..., 2, :] + value_bias).astype(jnp.bfloat16)
    key_masked = jnp.where(keep_all > 0, key_raw, -1e30)
    key_top = jnp.max(key_masked, axis=(0, 2), keepdims=True)
    expo = jnp.exp(key_masked - key_top)
    probs = expo / jnp.sum(expo, axis=(0, 2), keepdims=True)
    probs_low = probs.astype(jnp.bfloat16)
    split = (all_rows, image_count, col_count, heads_here, HD)
    query_heads = query.reshape(split)
    value_heads = value.reshape(split)
    probs_heads = probs_low.reshape(split)
    key_value = jnp.einsum(
        "yixha,yixhb->ihab", probs_heads, value_heads, preferred_element_type=jnp.float32
    ).astype(jnp.bfloat16)
    factored = jnp.einsum(
        "yixha,ihab->yixhb", query_heads, key_value, preferred_element_type=jnp.float32
    ) * HD ** (-0.5)
    query_full = query.astype(jnp.float32)
    value_pad = jnp.pad(value.astype(jnp.float32) * keep_all, ((3, 3), (0, 0), (3, 3), (0, 0)))
    near = depthwise(value_pad, near_kern, 3) + near_bias
    attended = (factored.reshape(query.shape) + query_full * near).astype(jnp.bfloat16)
    piece = attended
    second_sum = (
        first_sum
        + lax.psum_scatter(
            jnp.einsum("yixe,de->yixd", piece, proj_all, preferred_element_type=jnp.float32).astype(
                jnp.bfloat16
            ),
            "mp",
            scatter_dimension=0,
            tiled=True,
        ).astype(jnp.float32)
        + small_params[64]
    )
    normed_two, rstd_two = norm_parts(second_sum)
    mlp_in = (normed_two * small_params[65] + small_params[66]).astype(jnp.bfloat16)
    grad_out = cotangent * own_keep
    grad_low = grad_out.astype(jnp.bfloat16)
    mlp_all = lax.all_gather(mlp_in, "mp", axis=0, tiled=True)
    unit_bias = lax.dynamic_slice_in_dim(unit_bias_all, first_unit, hidden_width)
    hidden_pre = (
        jnp.einsum("yixd,df->yixf", mlp_all, expand_all, preferred_element_type=jnp.float32)
        + unit_bias
    )
    hidden_act = jax.nn.gelu(hidden_pre, approximate=False).astype(jnp.bfloat16)
    piece = hidden_act
    mlp_out = (
        lax.psum_scatter(
            jnp.einsum(
                "yixf,df->yixd", piece, contract_all, preferred_element_type=jnp.float32
            ).astype(jnp.bfloat16),
            "mp",
            scatter_dimension=0,
            tiled=True,
        ).astype(jnp.float32)
        + small_params[67]
    )
    grad_all = lax.all_gather(grad_low, "mp", axis=0, tiled=True)
    grad_contract = jnp.einsum(
        "yixd,yixf->df", grad_all, hidden_act, preferred_element_type=jnp.float32
    )
    grad_act = jnp.einsum(
        "yixd,df->yixf", grad_all, contract_all, preferred_element_type=jnp.float32
    )
    grad_pre = (grad_act * gelu_slope(hidden_pre)).astype(jnp.bfloat16)
    grad_expand = jnp.einsum("yixd,yixf->df", mlp_all, grad_pre, preferred_element_type=jnp.float32)
    unit_grads = lax.dynamic_update_slice_in_dim(
        jnp.zeros(unit_bias_all.shape, jnp.float32),
        cell_sums(grad_pre.astype(jnp.float32)),
        first_unit,
        0,
    )
    piece = grad_pre
    grad_norm_two = lax.psum_scatter(
        jnp.einsum("yixf,df->yixd", piece, expand_all, preferred_element_type=jnp.float32).astype(
            jnp.bfloat16
        ),
        "mp",
        scatter_dimension=0,
        tiled=True,
    ).astype(jnp.float32)
    block_out = (second_sum + mlp_out).astype(jnp.bfloat16)
    out_bias_grad = cell_sums(grad_low.astype(jnp.float32))
    gain_two_grad = cell_sums(grad_norm_two * normed_two)
    shift_two_grad = cell_sums(grad_norm_two)
    grad_second = grad_out + norm_back(grad_norm_two, normed_two, rstd_two, small_params[65])
    second_low = grad_second.astype(jnp.bfloat16)
    proj_bias_grad = cell_sums(second_low.astype(jnp.float32))
    second_all = lax.all_gather(second_low, "mp", axis=0, tiled=True)
    grad_proj = jnp.einsum(
        "yixd,yixe->de", second_all, attended, preferred_element_type=jnp.float32
    )
    grad_attended = jnp.einsum(
        "yixd,de->yixe", second_all, proj_all, preferred_element_type=jnp.float32
    ).astype(jnp.bfloat16)
    attended_heads = grad_attended.reshape(split)
    query_fact = jnp.einsum(
        "yixhb,ihab->yixha", attended_heads, key_value, preferred_element_type=jnp.float32
    ) * HD ** (-0.5)
    grad_kv = (
        jnp.einsum(
            "yixha,yixhb->ihab", query_heads, attended_heads, preferred_element_type=jnp.float32
        )
        * HD ** (-0.5)
    ).astype(jnp.bfloat16)
    grad_probs = jnp.einsum(
        "yixhb,ihab->yixha", value_heads, grad_kv, preferred_element_type=jnp.float32
    ).reshape(query.shape)
    grad_key = (
        probs * (grad_probs - jnp.sum(probs * grad_probs, axis=(0, 2), keepdims=True))
    ).astype(jnp.bfloat16)
    value_fact = jnp.einsum(
        "yixha,ihab->yixhb", probs_heads, grad_kv, preferred_element_type=jnp.float32
    ).reshape(query.shape)
    attended_full = grad_attended.astype(jnp.float32)
    grad_near = attended_full * query_full
    near_pad = jnp.pad(grad_near, ((3, 3), (0, 0), (3, 3), (0, 0)))
    value_near = transposed(near_pad, near_kern, 3) * keep_all
    near_taps = tap_sums(value_pad, grad_near, 3) * window
    grad_query = (query_fact.reshape(query.shape) + attended_full * near).astype(jnp.bfloat16)
    grad_value = (value_fact + value_near).astype(jnp.bfloat16)
    grad_kinds = jnp.stack([grad_query, grad_key, grad_value], axis=3)
    grad_qkv = jnp.einsum(
        "yixd,yixke->dke", attn_all, grad_kinds, preferred_element_type=jnp.float32
    )
    piece = grad_kinds
    grad_norm_one = lax.psum_scatter(
        jnp.einsum("yixke,dke->yixd", piece, qkv_all, preferred_element_type=jnp.float32).astype(
            jnp.bfloat16
        ),
        "mp",
        scatter_dimension=0,
        tiled=True,
    ).astype(jnp.float32)
    gain_one_grad = cell_sums(grad_norm_one * normed_one)
    shift_one_grad = cell_sums(grad_norm_one)
    grad_first = grad_second + norm_back(grad_norm_one, normed_one, rstd_one, small_params[59])
    first_edges = extended(grad_first.astype(jnp.bfloat16), (("mp", 0),), 1).astype(
        grad_first.dtype
    )
    first_pad = jnp.pad(first_edges, ((0, 0), (0, 0), (1, 1), (0, 0)))
    patch_grad = (grad_first + transposed(first_pad, cpe_kern, 1)) * own_keep
    cpe_taps = tap_sums(in_pad, grad_first, 1)

    def widen(vector):
        return lax.dynamic_update_slice_in_dim(
            jnp.zeros((channels,), jnp.float32), vector, first_chan, 0
        )

    near_rows = lax.dynamic_update_slice_in_dim(
        jnp.zeros((49, channels), jnp.float32), near_taps, first_chan, 1
    )
    vector_rows = jnp.stack(
        [
            cell_sums(grad_first),
            gain_one_grad,
            shift_one_grad,
            widen(cell_sums(grad_query.astype(jnp.float32))),
            widen(cell_sums(grad_value.astype(jnp.float32))),
            widen(cell_sums(grad_near)),
            proj_bias_grad,
            gain_two_grad,
            shift_two_grad,
            out_bias_grad,
        ]
    )
    small_local = jnp.concatenate(
        [cpe_taps, near_rows, vector_rows, unit_grads.reshape(-1, channels)], axis=0
    )
    grad_small = lax.psum(small_local, ("dp", "mp"))
    shard_qkv, shard_proj, shard_expand, shard_contract = side_by_side(
        (
            grad_qkv.astype(jnp.bfloat16),
            grad_proj.astype(jnp.bfloat16),
            grad_expand.astype(jnp.bfloat16),
            grad_contract.astype(jnp.bfloat16),
        ),
        "dp",
        0,
        1,
    )
    local_sq = (
        jnp.sum(shard_qkv * shard_qkv)
        + jnp.sum(shard_proj * shard_proj)
        + jnp.sum(shard_expand * shard_expand)
        + jnp.sum(shard_contract * shard_contract)
    )
    total_sq = lax.psum(local_sq, ("dp", "mp")) + jnp.sum(grad_small * grad_small)
    grad_norm = jnp.sqrt(total_sq)
    factor = jnp.minimum(1.0, CLIP_NORM / (grad_norm + 1e-06))
    rate_model = RATE_FACTOR * D ** (-0.5)
    rate_hidden = RATE_FACTOR * FF ** (-0.5)
    qkv_new = adamw(qkv_weight, qkv_mean, qkv_square, shard_qkv, factor, rate_model, WEIGHT_DECAY)
    proj_new = adamw(
        proj_weight, proj_mean, proj_square, shard_proj, factor, rate_model, WEIGHT_DECAY
    )
    expand_new = adamw(
        expand_weight, expand_mean, expand_square, shard_expand, factor, rate_model, WEIGHT_DECAY
    )
    contract_new = adamw(
        contract_weight,
        contract_mean,
        contract_square,
        shard_contract,
        factor,
        rate_hidden,
        WEIGHT_DECAY,
    )
    small_new = adamw(small_params, small_mean, small_square, grad_small, factor, SMALL_RATE, 0.0)
    return (
        block_out,
        patch_grad,
        grad_norm,
        qkv_new[0],
        qkv_new[1],
        qkv_new[2],
        proj_new[0],
        proj_new[1],
        proj_new[2],
        expand_new[0],
        expand_new[1],
        expand_new[2],
        contract_new[0],
        contract_new[1],
        contract_new[2],
        small_new[0],
        small_new[1],
        small_new[2],
    )


def solution(mesh):
    in_specs = (
        P("mp", "dp", None, None),
        P("mp", "dp", None, None),
        P("dp", None),
        P("dp", None, "mp"),
        P("dp", None, "mp"),
        P("dp", None, "mp"),
        P("dp", "mp"),
        P("dp", "mp"),
        P("dp", "mp"),
        P("dp", "mp"),
        P("dp", "mp"),
        P("dp", "mp"),
        P("dp", "mp"),
        P("dp", "mp"),
        P("dp", "mp"),
        P(),
        P(),
        P(),
    )
    out_specs = (
        P("mp", "dp", None, None),
        P("mp", "dp", None, None),
        P(),
        P("dp", None, "mp"),
        P("dp", None, "mp"),
        P("dp", None, "mp"),
        P("dp", "mp"),
        P("dp", "mp"),
        P("dp", "mp"),
        P("dp", "mp"),
        P("dp", "mp"),
        P("dp", "mp"),
        P("dp", "mp"),
        P("dp", "mp"),
        P("dp", "mp"),
        P(),
        P(),
        P(),
    )
    return jax.shard_map(
        on_device, mesh=mesh, in_specs=in_specs, out_specs=out_specs, check_vma=False
    )
```

profile of v0, /device:TPU:8, one launch (start us, length us, event | category | flops | bytes accessed | tf_op | source)
XLA Modules:
  0.0 874.3 jit_solution(9485794171534614168)
XLA Ops:
  23.6 28.1 %all_gather.26 = bf16[512,128]{1,0:T(8,128)(2,1)S(1)} all-gather(bf16[64,128]{1,0:T(8,128)(2,1)S(1)} %convert_element_type.197), channel_id=1, replica_groups=mesh['dp'=8,'mp'=4] {'dp'}, dimensions={0}, use_global_device_ids=true | all-gather | bytes 147456 | tf_op jit(solution)/shard_map/all_gather | solution.py:199
  51.8 31.7 %all_gather.25 = bf16[512,3,128]{2,0,1:T(8,128)(2,1)S(1)} all-gather(bf16[64,3,128]{2,0,1:T(8,128)(2,1)S(1)} %convert_element_type.187), channel_id=1, replica_groups=mesh['dp'=8,'mp'=4] {'dp'}, dimensions={0}, use_global_device_ids=true | all-gather | bytes 442368 | tf_op jit(solution)/shard_map/all_gather | solution.py:198
  116.8 6.3 fusion.219
  136.1 53.9 %fusion.43 = (bf16[16,8,32,128]{3,2,1,0:T(8,128)(2,1)S(1)}, f32[16,8,32,128]{3,2,1,0:T(8,128)}) fusion(f32[16,8,32,128]{3,2,1,0:T(8,128)} %reshape.359, f32[128]{0:T(128)} %get-tuple-element.242, f32[16,8,32,3,128]{4,2,3,1,0:T(8,128)} %copy-done.2, f32[128]{0:T(128)S(1)} %fusion.251, f32[128]{0:T(128)} %get-tuple-element.190, f32[128]{0:T(128)} %get-tuple-element.191, ...), kind=kLoop, calls=%fused_computation.189 | loop fusion | flops 54525952 | bytes 9463296 | tf_op jit(solution)/shard_map/convert_element_type | solution.py:234
  194.2 51.1 %reduce-scatter.5.cloned.1.call-done = bf16[4,8,32,512]{3,2,1,0:T(8,128)(2,1)} async-done(((bf16[16,8,32,512]{3,2,1,0:T(8,128)(2,1)}), bf16[4,8,32,512]{3,2,1,0:T(8,128)(2,1)}) %reduce-scatter.5.cloned.1.call-update) | async-done | bytes 1048592 | tf_op jit(solution)/shard_map/reduce_scatter | solution.py:238
  252.3 28.7 %all_gather.29 = bf16[512,512]{1,0:T(8,128)(2,1)S(1)} all-gather(bf16[64,512]{1,0:T(8,128)(2,1)S(1)} %convert_element_type.203), channel_id=1, replica_groups=mesh['dp'=8,'mp'=4] {'dp'}, dimensions={0}, use_global_device_ids=true | all-gather | bytes 589824 | tf_op jit(solution)/shard_map/all_gather | solution.py:201
  281.0 31.2 %all_gather.28 = bf16[512,512]{1,0:T(8,128)(2,1)S(1)} all-gather(bf16[64,512]{1,0:T(8,128)(2,1)S(1)} %convert_element_type.201), channel_id=1, replica_groups=mesh['dp'=8,'mp'=4] {'dp'}, dimensions={0}, use_global_device_ids=true | all-gather | bytes 589824 | tf_op jit(solution)/shard_map/all_gather | solution.py:200
  312.2 8.5 fusion.33
  320.7 8.8 %convert_reduce_fusion = (f32[512]{0:T(512)}, bf16[16,8,32,512]{3,2,1,0:T(8,128)(2,1)S(1)}) fusion(f32[16,8,32,512]{3,2,1,0:T(8,128)} %get-tuple-element.248, f32[512]{0:T(512)S(1)} %dynamic_slice.19, bf16[16,8,32,512]{3,2,1,0:T(8,128)(2,1)} %all-gather.9.cloned.1.call-done, bf16[512,512]{1,0:T(8,128)(2,1)S(1)} %all_gather.29), kind=kOutput, calls=%fused_computation.113 | convolution fusion | flops 2174746112 | bytes 17305600 | tf_op jit(solution)/shard_map/yixd,df->yixf/dot_general | solution.py:275
  336.8 20.3 %fusion.2 = bf16[16,8,32,512]{3,2,1,0:T(8,128)(2,1)S(1)} fusion(f32[16,8,32,512]{3,2,1,0:T(8,128)} %get-tuple-element.248, f32[512]{0:T(512)S(1)} %dynamic_slice.19, u16[8,32,512]{2,1,0:T(8,128)(2,1)S(1)} %get-tuple-element.55, u16[8,32,512]{2,1,0:T(8,128)(2,1)S(1)} %get-tuple-element.54), kind=kLoop, calls=%fused_computation.100 | loop fusion | flops 148897792 | bytes 13109248 | tf_op jit(solution)/shard_map/convert_element_type | solution.py:258
  363.7 20.2 %reduce-scatter.9.cloned.1.call-done = bf16[4,8,32,512]{3,2,1,0:T(8,128)(2,1)} async-done(((bf16[16,8,32,512]{3,2,1,0:T(8,128)(2,1)}), bf16[4,8,32,512]{3,2,1,0:T(8,128)(2,1)}) %reduce-scatter.9.cloned.1.call-update) | async-done | bytes 1048592 | tf_op jit(solution)/shard_map/reduce_scatter | solution.py:287
  388.2 42.6 %reduce-scatter.7.cloned.1.call-done = bf16[4,8,32,512]{3,2,1,0:T(8,128)(2,1)} async-done(((bf16[16,8,32,512]{3,2,1,0:T(8,128)(2,1)}), bf16[4,8,32,512]{3,2,1,0:T(8,128)(2,1)}) %reduce-scatter.7.cloned.1.call-update) | async-done | bytes 1048592 | tf_op jit(solution)/shard_map/reduce_scatter | solution.py:261
  435.2 6.7 fusion.187
  441.9 27.9 %all-gather.11.cloned.1.call-done = bf16[16,8,32,512]{3,2,1,0:T(8,128)(2,1)} async-done(((bf16[4,8,32,512]{3,2,1,0:T(8,128)(2,1)}), bf16[16,8,32,512]{3,2,1,0:T(8,128)(2,1)}) %all-gather.11.cloned.1.call-update) | async-done | bytes 4194320 | tf_op jit(solution)/shard_map/all_gather | solution.py:302
  469.8 8.5 multiply_reduce_fusion.1
  507.9 8.2 copy.126
  521.5 8.3 copy.128
  535.6 56.3 %convert_reduce_fusion.6 = (f32[128]{0:T(128)}, bf16[16,8,32,128]{3,2,1,0:T(8,128)(2,1)S(1)}) fusion(f32[16,8,32,128]{3,2,1,0:T(8,128)} %reshape.364, f32[16,8,32]{2,1,0:T(8,128)} %copy-done.32, f32[128]{0:T(128)} %get-tuple-element.190, f32[128]{0:T(128)} %get-tuple-element.191, f32[128]{0:T(128)} %get-tuple-element.192, f32[128]{0:T(128)} %get-tuple-element.193, ...), kind=kLoop, calls=%fused_computation.327 | loop fusion | flops 53477248 | bytes 5284864 | tf_op jit(solution)/shard_map/reduce_sum | solution.py:128
  601.7 6.7 fusion.192
  638.0 21.5 %all-to-all-done = bf16[8,64,1536]{2,1,0:T(8,128)(2,1)} async-done(((bf16[8,64,1536]{2,1,0:T(8,128)(2,1)}), bf16[8,64,1536]{2,1,0:T(8,128)(2,1)}, u32[]{:S(2)}, u32[]{:S(2)}) %all-to-all-start) | async-done | bytes 1572896 | tf_op jit(solution)/shard_map/all_to_all | solution.py:50
  667.5 40.4 %psum.14 = f32[]{:T(128)} all-reduce(f32[]{:T(128)S(6)} %add.821), channel_id=1, replica_groups=mesh['dp'=8,'mp'=4] {'dp','mp'}, use_global_device_ids=true, to_apply=%region_20.21 | all-reduce | flops 1 | bytes 8 | tf_op jit(solution)/shard_map/psum | solution.py:401
  711.6 8.3 multiply_reduce_fusion.50
  719.9 7.0 concatenate.28
  731.7 119.1 %all-reduce.6.cloned.1.call-done = f32[72,512]{1,0:T(8,128)} async-done(((f32[72,512]{1,0:T(8,128)}), f32[72,512]{1,0:T(8,128)}) %all-reduce.6.cloned.1.call-update) | async-done | bytes 147472 | tf_op jit(solution)/shard_map/psum | solution.py:383
  (441 shorter events, 202.5 us)
Async XLA Ops:
  7.2 77.9 %all-gather.5.cloned.1.call-start = ((), (), s32[]{:S(2)}) async-start(), calls=%async_computation.5 | async-start | bytes 5242880 | tf_op jit(solution)/shard_map/all_gather | solution.py:211
  8.2 241.7 %copy-start.40 = (f32[4,8,32]{2,1,0:T(8,128)}, f32[4,8,32]{2,1,0:T(8,128)S(1)}, u32[]{:S(2)}) copy-start(f32[4,8,32]{2,1,0:T(8,128)S(1)} %get-tuple-element.244) | copy-start | bytes 12292
  9.7 3.8 collective-permute-start
  11.5 4.7 collective-permute-start.1
  13.5 233.9 %copy-start.62 = (f32[1,512]{1,0:T(1,128)}, f32[1,512]{1,0:T(1,128)S(1)}, u32[]{:S(2)}) copy-start(f32[1,512]{1,0:T(1,128)S(1)} %get-tuple-element.172) | copy-start | bytes 6148
  19.6 225.7 %copy-start.3 = (f32[4,8,32,512]{3,2,1,0:T(8,128)}, f32[4,8,32,512]{3,2,1,0:T(8,128)S(1)}, u32[]{:S(2)}) copy-start(f32[4,8,32,512]{3,2,1,0:T(8,128)S(1)} %get-tuple-element.156) | copy-start | bytes 6291460
  21.5 223.8 %reduce-scatter.5.cloned.1.call-start = ((), (), s32[]{:S(2)}) async-start(), calls=%async_computation.6 | async-start | bytes 5242880 | tf_op jit(solution)/shard_map/reduce_scatter | solution.py:238
  51.8 138.2 %copy-start.39 = (bf16[512,128]{1,0:T(8,128)(2,1)}, bf16[512,128]{1,0:T(8,128)(2,1)S(1)}, u32[]{:S(2)}) copy-start(bf16[512,128]{1,0:T(8,128)(2,1)S(1)} %all_gather.26) | copy-start | bytes 393220
  194.2 118.1 %all-gather.7.cloned.1.call-start = ((), (), s32[]{:S(2)}) async-start(), calls=%async_computation.7 | async-start | bytes 5242880 | tf_op jit(solution)/shard_map/all_gather | solution.py:252
  249.7 71.0 %all-gather.9.cloned.1.call-start = ((), (), s32[]{:S(2)}) async-start(), calls=%async_computation.9 | async-start | bytes 5242880 | tf_op jit(solution)/shard_map/all_gather | solution.py:271
  252.1 131.8 %reduce-scatter.9.cloned.1.call-start = ((), (), s32[]{:S(2)}) async-start(), calls=%async_computation.10 | async-start | bytes 5242880 | tf_op jit(solution)/shard_map/reduce_scatter | solution.py:287
  336.3 94.5 %reduce-scatter.7.cloned.1.call-start = ((), (), s32[]{:S(2)}) async-start(), calls=%async_computation.8 | async-start | bytes 5242880 | tf_op jit(solution)/shard_map/reduce_scatter | solution.py:261
  363.7 106.1 %all-gather.11.cloned.1.call-start = ((), (), s32[]{:S(2)}) async-start(), calls=%async_computation.11 | async-start | bytes 5242880 | tf_op jit(solution)/shard_map/all_gather | solution.py:302
  435.1 272.7 %reduce-scatter.11.cloned.1.call-start = ((), (), s32[]{:S(2)}) async-start(), calls=%async_computation.12 | async-start | bytes 5242880 | tf_op jit(solution)/shard_map/reduce_scatter | solution.py:340
  618.3 41.1 %all-to-all-start = ((bf16[8,64,1536]{2,1,0:T(8,128)(2,1)}), bf16[8,64,1536]{2,1,0:T(8,128)(2,1)}, u32[]{:S(2)}, u32[]{:S(2)}) async-start(bf16[8,64,1536]{2,1,0:T(8,128)(2,1)} %pad_maximum_fusion.1), calls=%async_computation.4 | async-start | bytes 3145728 | tf_op jit(solution)/shard_map/all_to_all | solution.py:50
  624.5 226.3 %all-reduce.6.cloned.1.call-start = ((), (), s32[]{:S(2)}) async-start(), calls=%async_computation.13 | async-start | bytes 294912 | tf_op jit(solution)/shard_map/psum | solution.py:383
  727.0 129.1 %copy-start.31 = (f32[72,512]{1,0:T(8,128)S(1)}, f32[72,512]{1,0:T(8,128)}, u32[]{:S(2)}) copy-start(f32[72,512]{1,0:T(8,128)} %param.33) | copy-start | bytes 442372
  727.0 129.1 %copy-start.55 = (f32[72,512]{1,0:T(8,128)S(1)}, f32[72,512]{1,0:T(8,128)}, u32[]{:S(2)}) copy-start(f32[72,512]{1,0:T(8,128)} %param.34) | copy-start | bytes 442372
  727.0 129.1 %copy-start.56 = (f32[72,512]{1,0:T(8,128)S(1)}, f32[72,512]{1,0:T(8,128)}, u32[]{:S(2)}) copy-start(f32[72,512]{1,0:T(8,128)} %param.35) | copy-start | bytes 442372
  728.9 129.0 %copy-start.36 = (f32[64,512]{1,0:T(8,128)S(1)}, f32[64,512]{1,0:T(8,128)}, u32[]{:S(2)}) copy-start(f32[64,512]{1,0:T(8,128)} %param.27) | copy-start | bytes 393220
  728.9 129.0 %copy-start.38 = (f32[64,512]{1,0:T(8,128)S(1)}, f32[64,512]{1,0:T(8,128)}, u32[]{:S(2)}) copy-start(f32[64,512]{1,0:T(8,128)} %param.30) | copy-start | bytes 393220
  728.9 128.9 %copy-start.59 = (f32[64,512]{1,0:T(8,128)S(1)}, f32[64,512]{1,0:T(8,128)}, u32[]{:S(2)}) copy-start(f32[64,512]{1,0:T(8,128)} %param.31) | copy-start | bytes 393220
  729.0 131.0 %collective-permute-start.2 = (bf16[1,8,32,512]{3,2,1,0:T(8,128)(2,1)S(1)}, bf16[1,8,32,512]{3,2,1,0:T(8,128)(2,1)S(1)}, u32[]{:S(2)}, u32[]{:S(2)}) collective-permute-start(bf16[1,8,32,512]{3,2,1,0:T(8,128)(2,1)S(1)} %get-tuple-element.163), channel_id=1, source_target_pairs={{0,1},{1,2},{2,3},{4,5},{5,6},{6,7},{8,9},{9,10},{10,11},{12,13},{... | collective-permute-start | bytes 786440 | tf_op jit(solution)/shard_map/ppermute | solution.py:34
  730.4 129.6 %collective-permute-start.3 = (bf16[1,8,32,512]{3,2,1,0:T(8,128)(2,1)S(1)}, bf16[1,8,32,512]{3,2,1,0:T(8,128)(2,1)S(1)}, u32[]{:S(2)}, u32[]{:S(2)}) collective-permute-start(bf16[1,8,32,512]{3,2,1,0:T(8,128)(2,1)S(1)} %get-tuple-element.164), channel_id=1, source_target_pairs={{1,0},{2,1},{3,2},{5,4},{6,5},{7,6},{9,8},{10,9},{11,10},{13,12},{... | collective-permute-start | bytes 786440 | tf_op jit(solution)/shard_map/ppermute | solution.py:36
  (140 other events, 2893.0 us)
Sparse Core Ops, SparseCore 0:
  21.6 39.1 all-gather.4
  194.3 51.0 reduce-scatter.4
  249.8 34.4 all-gather.6
  285.8 34.4 all-gather.8
  336.4 47.4 reduce-scatter.8
  386.3 44.4 reduce-scatter.6
  435.2 34.4 all-gather.10
  601.8 44.5 reduce-scatter.10
  727.1 123.6 all-reduce.5
where the time goes:
time: 879 us; the launch traced here: 874 us
  waiting for transfers between devices  285 us (32%)
  other arithmetic  202 us (23%)
  blocking collectives  160 us (18%)
  local copies, waits for them, and re-layouts  106 us (12%)
  matrix products  86.9 us (10%)
  between operations  21.4 us (2%)
  starting transfers between devices  12.9 us (1%)
    psum x1, waiting for transfers between devices, on_device(): grad_small = lax.psum(small_local, ('dp', 'mp'))  119 us
    reduce_sum x6, other arithmetic, cell_sums(): return jnp.sum(values, axis=(0, 1, 2))  70.4 us
    convert_element_type x1, other arithmetic, on_device(): (factored.reshape(query.shape) + query_full * near).astype(jnp.bfloat16)  53.9 us
    reduce_scatter x1, waiting for transfers between devices, on_device(): lax.psum_scatter(jnp.einsum('yixe,de->yixd', piece, proj_all, preferred_e...  51.1 us
    reduce_scatter x1, waiting for transfers between devices, on_device(): lax.psum_scatter(jnp.einsum('yixf,df->yixd', piece, contract_all, preferr...  42.6 us
    psum x1, blocking collectives, on_device(): lax.psum(local_sq, ('dp', 'mp')) + jnp.sum(grad_small * grad_small)  40.4 us
    all_gather x1, blocking collectives, on_device(): lax.all_gather(qkv_weight.astype(jnp.bfloat16), 'dp', axis=0, tiled=True)  31.7 us
    all_gather x1, blocking collectives, on_device(): lax.all_gather(expand_weight.astype(jnp.bfloat16), 'dp', axis=0, tiled=True)  31.2 us
  transfers between devices with their start and end apart: 14, of which 7 were waited for; matrix products, arithmetic and copies ran while one was open for 11% of the time, Pallas kernels for 0%

commit v1 on v0

v1 whole, which is shorter than its diff:
```python
import functools
import math

import jax
import jax.numpy as jnp
from jax import lax
from jax.experimental import pallas as pl
from jax.experimental.pallas import tpu as pltpu
from jax.sharding import PartitionSpec as P

D = 512
HD = 64
FF = 2048
STEP = 10


NORM_EPS = 1e-06
CLIP_NORM = 1.0
BETA_ONE = 0.9
BETA_TWO = 0.999
ADAM_EPS = 1e-08
WEIGHT_DECAY = 0.05
RATE_FACTOR = 2.0
SMALL_RATE = 0.5
ROOT_HALF = 0.7071067811865476
INV_ROOT_TAU = 0.3989422804014327
HEAD_SCALE = HD ** (-0.5)

LANES = 128
SUB = 8
VMEM_LIMIT = 60 * 1024 * 1024
F32 = jnp.float32
BF16 = jnp.bfloat16


def radius_of(head):
    return 1 if head < 2 else 2 if head < 5 else 3


def log2(size):
    bits = size.bit_length() - 1
    assert 1 << bits == size
    return bits


def flip(array, axis, bit):
    size = lax.axis_size(axis)
    return lax.ppermute(array, axis, [(i, i ^ (1 << bit)) for i in range(size)])


def bit_of(axis, bit):
    return (lax.axis_index(axis) >> bit) & 1


def gathered(array, axis):
    array = array[None]
    for bit in range(log2(lax.axis_size(axis))):
        other = flip(array, axis, bit)
        upper = bit_of(axis, bit) == 1
        array = jnp.where(
            upper,
            jnp.concatenate([other, array], axis=0),
            jnp.concatenate([array, other], axis=0),
        )
    return array


def halved(array, axis, dim):
    size = lax.axis_size(axis)
    bits = log2(size)
    before, after = array.shape[:dim], array.shape[dim + 1 :]
    array = array.reshape(*before, *([2] * bits), *after)
    for bit in range(bits):
        place = dim + bits - 1 - bit
        mine = lax.dynamic_index_in_dim(array, bit_of(axis, bit), place, keepdims=False)
        theirs = lax.dynamic_index_in_dim(array, 1 - bit_of(axis, bit), place, keepdims=False)
        got = flip(theirs, axis, bit)
        array = (mine.astype(F32) + got.astype(F32)).astype(array.dtype)
    return array


def to_images(cells):
    size = lax.axis_size("mp")
    rows, images, cols, channels = cells.shape
    tiles = cells.reshape(rows, size, images // size, cols, channels).transpose(1, 0, 2, 3, 4)
    tiles = lax.all_to_all(tiles, "mp", 0, 0, tiled=True)
    return tiles.transpose(2, 0, 1, 3, 4).reshape(images // size, size * rows, cols, channels)


def to_rows(cells):
    size = lax.axis_size("mp")
    images, rows, cols, channels = cells.shape
    tiles = cells.reshape(images, size, rows // size, cols, channels).transpose(1, 0, 2, 3, 4)
    tiles = lax.all_to_all(tiles, "mp", 0, 0, tiled=True)
    return tiles.transpose(2, 0, 1, 3, 4).reshape(rows // size, size * images, cols, channels)


def dot(a, b):
    return lax.dot_general(a, b, (((1,), (0,)), ((), ())), preferred_element_type=F32)


def dot_rt(a, b):
    return lax.dot_general(a, b, (((1,), (1,)), ((), ())), preferred_element_type=F32)


def dot_lt(a, b):
    return lax.dot_general(a, b, (((0,), (0,)), ((), ())), preferred_element_type=F32)


def row_mean(values):
    return jnp.sum(values, axis=-1, keepdims=True) * (1.0 / values.shape[-1])


def norm_parts(values):
    center = values - row_mean(values)
    rstd = lax.rsqrt(row_mean(center * center) + NORM_EPS)
    return center * rstd, rstd


def norm_back(gradient, normed, rstd, gain_row):
    scaled = gradient * gain_row
    return rstd * (scaled - row_mean(scaled) - normed * row_mean(scaled * normed))


def shifted_rows(src, lead, rows, start, lanes=slice(None)):
    return [src[lead, y, pl.ds(start, SUB), lanes] for y in range(rows)]


def filtered(src, lead, rows, col, taps, radius, sign, lanes=slice(None)):
    acc = [None] * rows
    for dx in range(-radius, radius + 1):
        cells = shifted_rows(src, lead, rows, col + SUB + sign * dx, lanes)
        for dy in range(-radius, radius + 1):
            tap = taps(dy, dx)
            for y in range(rows):
                from_row = y + sign * dy
                if 0 <= from_row < rows:
                    term = tap * cells[from_row]
                    acc[y] = term if acc[y] is None else acc[y] + term
    return acc


def tap_products(src, own, images, rows, cols, dx, radius, lanes=slice(None)):
    def image(lead, acc):
        acc = list(acc)
        for col in range(0, cols, SUB):
            cells = shifted_rows(src, lead, rows, col + SUB - dx, lanes)
            mine = [own(lead, y, col) for y in range(rows)]
            for k, dy in enumerate(range(-radius, radius + 1)):
                total = acc[k]
                for y in range(rows):
                    if 0 <= y - dy < rows:
                        total = total + mine[y] * cells[y - dy]
                acc[k] = total
        return tuple(acc)

    zero = jnp.zeros((SUB, LANES), F32)
    return lax.fori_loop(0, images, image, (zero,) * (2 * radius + 1))


def loop(count, body):
    def step(i, carry):
        body(i)
        return carry

    lax.fori_loop(0, count, step, 0)


def col_keep(shape_ref, lead, cols, lanes):
    return lax.broadcasted_iota(jnp.int32, (cols, lanes), 0) < shape_ref[lead, 1]


def cell_keep(shape_ref, lead, rows, cols, lanes):
    x = lax.broadcasted_iota(jnp.int32, (rows, cols, lanes), 1)
    y = lax.broadcasted_iota(jnp.int32, (rows, cols, lanes), 0)
    kept = (x < shape_ref[lead, 1]) & (y < shape_ref[lead, 0])
    return kept.reshape(rows * cols, lanes)


def head_diagonal():
    a = lax.broadcasted_iota(jnp.int32, (LANES, LANES), 0) // HD
    b = lax.broadcasted_iota(jnp.int32, (LANES, LANES), 1) // HD
    return a == b


def by_radius(step, radii, run):
    for radius in sorted(set(radii)):
        steps = [k for k, r in enumerate(radii) if r == radius]
        hit = functools.reduce(lambda a, b: a | b, [step == k for k in steps])
        pl.when(hit)(functools.partial(run, radius))


def attention_kernel(
    dims,
    radii,
    shape_ref,
    x_ref,
    small_ref,
    part_ref,
    wq_ref,
    wp_ref,
    first_ref,
    norma_ref,
    query_ref,
    probs_ref,
    value_ref,
    near_ref,
    attended_ref,
    kv_ref,
    second_ref,
    normb_ref,
    pad_x,
    pad_v,
    near_f,
    total,
):
    images, rows, cols, channels = dims
    cells = rows * cols
    step = pl.program_id(0)
    last = pl.num_programs(0) - 1

    @pl.when(step == 0)
    def _():
        pad_x[...] = jnp.zeros_like(pad_x)
        pad_v[...] = jnp.zeros_like(pad_v)

        def mask_row(r):
            lead = r // rows
            y = r % rows
            kept = col_keep(shape_ref, lead, cols, channels) & (y < shape_ref[lead, 0])
            block = x_ref[pl.ds(pl.multiple_of(r * cols, cols), cols), :].astype(F32)
            pad_x[lead, y, pl.ds(SUB, cols), :] = jnp.where(kept, block, 0.0)

        loop(images * rows, mask_row)

        def conv(lead):
            for lane in range(0, channels, LANES):
                lanes = pl.ds(lane, LANES)
                for col in range(0, cols, SUB):
                    out = filtered(
                        pad_x,
                        lead,
                        rows,
                        col,
                        lambda dy, dx: small_ref[pl.ds(3 * (dy + 1) + dx + 1, 1), lanes],
                        1,
                        1,
                        lanes,
                    )
                    bias = small_ref[pl.ds(58, 1), lanes]
                    for y in range(rows):
                        own = pad_x[lead, y, pl.ds(SUB + col, SUB), lanes]
                        at = pl.multiple_of(lead * cells + (y * cols + col), SUB)
                        first_ref[pl.ds(at, SUB), lanes] = own + out[y] + bias

        loop(images, conv)

        def normalize(r):
            at = pl.ds(pl.multiple_of(r * cols, cols), cols)
            normed, _ = norm_parts(first_ref[at, :])
            norma_ref[at, :] = (
                normed * small_ref[pl.ds(59, 1), :] + small_ref[pl.ds(60, 1), :]
            ).astype(BF16)

        loop(images * rows, normalize)

    diagonal = head_diagonal()

    def project(lead):
        at = pl.ds(pl.multiple_of(lead * cells, cells), cells)
        proj = dot(norma_ref[at, :], wq_ref[0])
        query = (proj[:, :LANES] + part_ref[0, pl.ds(61, 1), :]).astype(BF16)
        value = (proj[:, 2 * LANES :] + part_ref[0, pl.ds(62, 1), :]).astype(BF16)
        kept = cell_keep(shape_ref, lead, rows, cols, LANES)
        key = jnp.where(kept, proj[:, LANES : 2 * LANES], -1e30)
        expo = jnp.exp(key - jnp.max(key, axis=0, keepdims=True))
        probs = (expo / jnp.sum(expo, axis=0, keepdims=True)).astype(BF16)
        query_ref[0, at, :] = query
        probs_ref[0, at, :] = probs
        value_ref[0, at, :] = value
        kv = jnp.where(diagonal, dot_lt(probs, value), 0.0).astype(BF16)
        kv_ref[0, lead] = kv
        masked = jnp.where(kept, value.astype(F32), 0.0)
        pad_v[lead, :, pl.ds(SUB, cols), :] = masked.reshape(rows, cols, LANES)

    loop(images, project)

    def conv_near(radius):
        def conv(lead):
            for col in range(0, cols, SUB):
                out = filtered(
                    pad_v,
                    lead,
                    rows,
                    col,
                    lambda dy, dx: part_ref[0, pl.ds(9 + 7 * (dy + 3) + dx + 3, 1), :],
                    radius,
                    1,
                )
                bias = part_ref[0, pl.ds(63, 1), :]
                for y in range(rows):
                    at = pl.multiple_of(lead * cells + (y * cols + col), SUB)
                    near_f[pl.ds(at, SUB), :] = out[y] + bias

        loop(images, conv)

    by_radius(step, radii, conv_near)

    def attend(lead):
        at = pl.ds(pl.multiple_of(lead * cells, cells), cells)
        query = query_ref[0, at, :]
        near = near_f[at, :]
        near_ref[0, at, :] = near.astype(BF16)
        factored = dot(query, kv_ref[0, lead]) * HEAD_SCALE
        attended = (factored + query.astype(F32) * near).astype(BF16)
        attended_ref[0, at, :] = attended
        out = dot_rt(attended, wp_ref[0])

        @pl.when(step == 0)
        def _():
            total[at, :] = out

        @pl.when(step > 0)
        def _():
            total[at, :] = total[at, :] + out

    loop(images, attend)

    @pl.when(step == last)
    def _():
        def finish(r):
            at = pl.ds(pl.multiple_of(r * cols, cols), cols)
            second = first_ref[at, :] + total[at, :] + small_ref[pl.ds(64, 1), :]
            second_ref[at, :] = second
            normed, _ = norm_parts(second)
            normb_ref[at, :] = (
                normed * small_ref[pl.ds(65, 1), :] + small_ref[pl.ds(66, 1), :]
            ).astype(BF16)

        loop(images * rows, finish)


def gelu_parts(pre):
    cdf = 0.5 * (1.0 + lax.erf(pre * ROOT_HALF))
    return pre * cdf, cdf + pre * (jnp.exp(-0.5 * pre * pre) * INV_ROOT_TAU)


def hidden_kernel(
    dims,
    shape_ref,
    cot_ref,
    normb_ref,
    second_ref,
    small_ref,
    bias_ref,
    w1_ref,
    w2_ref,
    out_ref,
    dsecond_ref,
    dw_ref,
    dbias_ref,
    sums_ref,
    dout,
    pre,
    act_grad,
    hact,
    dhpre,
    total,
    dnorm,
):
    images, rows, cols, channels = dims
    cells = rows * cols
    step = pl.program_id(0)
    last = pl.num_programs(0) - 1
    hidden = w1_ref.shape[2]

    @pl.when(step == 0)
    def _():
        def mask_row(r):
            lead = r // rows
            y = r % rows
            kept = col_keep(shape_ref, lead, cols, channels) & (y < shape_ref[lead, 0])
            at = pl.ds(pl.multiple_of(r * cols, cols), cols)
            block = cot_ref[at, :].astype(F32)
            dout[at, :] = jnp.where(kept, block, 0.0).astype(BF16)

        loop(images * rows, mask_row)

    dbias_ref[...] = jnp.zeros_like(dbias_ref)

    def tile(lead):
        at = pl.ds(pl.multiple_of(lead * cells, cells), cells)
        pre[...] = dot(normb_ref[at, :], w1_ref[0]) + bias_ref[0]
        act_grad[...] = dot(dout[at, :], w2_ref[0])

        def chunk(r, acc):
            here = pl.ds(pl.multiple_of(r * 16, 16), 16)
            there = pl.ds(pl.multiple_of(lead * cells + r * 16, 16), 16)
            act, slope = gelu_parts(pre[here, :])
            hact[there, :] = act.astype(BF16)
            back = (act_grad[here, :] * slope).astype(BF16)
            dhpre[there, :] = back
            return acc + back.astype(F32)

        acc = lax.fori_loop(0, cells // 16, chunk, jnp.zeros((16, hidden), F32))
        dbias_ref[0] = dbias_ref[0] + jnp.sum(acc, axis=0, keepdims=True)
        out = dot_rt(hact[at, :], w2_ref[0])
        back = dot_rt(dhpre[at, :], w1_ref[0])

        @pl.when(step == 0)
        def _():
            total[at, :] = out
            dnorm[at, :] = back

        @pl.when(step > 0)
        def _():
            total[at, :] = total[at, :] + out
            dnorm[at, :] = dnorm[at, :] + back

    loop(images, tile)
    dw_ref[0, :, :hidden] = dot_lt(normb_ref[...], dhpre[...]).astype(BF16)
    dw_ref[0, :, hidden:] = dot_lt(dout[...], hact[...]).astype(BF16)

    @pl.when(step == last)
    def _():
        gain = small_ref[pl.ds(65, 1), :]

        def finish(r, acc):
            at = pl.ds(pl.multiple_of(r * cols, cols), cols)
            second = second_ref[at, :]
            out_ref[at, :] = (second + total[at, :] + small_ref[pl.ds(67, 1), :]).astype(BF16)
            normed, rstd = norm_parts(second)
            back = dnorm[at, :]
            got = dout[at, :].astype(F32)
            dsecond = got + norm_back(back, normed, rstd, gain)
            dsecond_ref[at, :] = dsecond
            low = dsecond.astype(BF16).astype(F32)
            terms = (low, back * normed, back, got)
            return tuple(
                a + jnp.sum(t.reshape(cols // SUB, SUB, channels), axis=0)
                for a, t in zip(acc, terms)
            )

        zero = jnp.zeros((SUB, channels), F32)
        acc = lax.fori_loop(0, images * rows, finish, (zero,) * 4)
        sums_ref[...] = jnp.zeros_like(sums_ref)
        for k, a in enumerate(acc):
            sums_ref[pl.ds(k, 1), :] = jnp.sum(a, axis=0, keepdims=True)


def attention_back_kernel(
    dims,
    radii,
    shape_ref,
    dsecond_ref,
    norma_ref,
    part_ref,
    wq_ref,
    wp_ref,
    query_ref,
    probs_ref,
    value_ref,
    near_ref,
    attended_ref,
    kv_ref,
    dnorma_ref,
    dw_ref,
    sums_ref,
    low,
    pad_d,
    value_f,
    grads,
    dvalue_f,
):
    images, rows, cols, channels = dims
    cells = rows * cols
    step = pl.program_id(0)

    @pl.when(step == 0)
    def _():
        pad_d[...] = jnp.zeros_like(pad_d)

        def round_row(r):
            at = pl.ds(pl.multiple_of(r * cols, cols), cols)
            low[at, :] = dsecond_ref[at, :].astype(BF16)

        loop(images * rows, round_row)

    sums_ref[...] = jnp.zeros_like(sums_ref)
    diagonal = head_diagonal()

    def first_half(lead):
        at = pl.ds(pl.multiple_of(lead * cells, cells), cells)
        datt = dot(low[at, :], wp_ref[0]).astype(BF16)
        query = query_ref[0, at, :]
        probs = probs_ref[0, at, :]
        value = value_ref[0, at, :]
        kept = cell_keep(shape_ref, lead, rows, cols, LANES)
        dkv = jnp.where(diagonal, dot_lt(query, datt) * HEAD_SCALE, 0.0).astype(BF16)
        datt_f = datt.astype(F32)
        dnear = datt_f * query.astype(F32)
        pad_d[lead, :, pl.ds(SUB, cols), :] = dnear.reshape(rows, cols, LANES)
        dquery = (
            dot_rt(datt, kv_ref[0, lead]) * HEAD_SCALE + datt_f * near_ref[0, at, :].astype(F32)
        ).astype(BF16)
        dprobs = dot_rt(value, dkv)
        probs_f = probs.astype(F32)
        inner = jnp.sum(probs_f * dprobs, axis=0, keepdims=True)
        dkey = (probs_f * (dprobs - inner)).astype(BF16)
        grads[at, :LANES] = dquery
        grads[at, LANES : 2 * LANES] = dkey
        dvalue_f[at, :] = dot(probs, dkv)
        value_f[at, :] = jnp.where(kept, value.astype(F32), 0.0)
        sums_ref[0, pl.ds(61, 1), :] += jnp.sum(dquery.astype(F32), axis=0, keepdims=True)
        sums_ref[0, pl.ds(63, 1), :] += jnp.sum(dnear, axis=0, keepdims=True)

    loop(images, first_half)

    def conv_back(radius):
        def conv(lead):
            x = lax.broadcasted_iota(jnp.int32, (SUB, LANES), 0)
            for col in range(0, cols, SUB):
                out = filtered(
                    pad_d,
                    lead,
                    rows,
                    col,
                    lambda dy, dx: part_ref[0, pl.ds(9 + 7 * (dy + 3) + dx + 3, 1), :],
                    radius,
                    -1,
                )
                inside = (x + col) < shape_ref[lead, 1]
                for y in range(rows):
                    at = pl.ds(pl.multiple_of(lead * cells + (y * cols + col), SUB), SUB)
                    kept = inside & (y < shape_ref[lead, 0])
                    dvalue_f[at, :] = dvalue_f[at, :] + jnp.where(kept, out[y], 0.0)

        loop(images, conv)

        def own(lead, y, col):
            at = pl.multiple_of(lead * cells + (y * cols + col), SUB)
            return value_f[pl.ds(at, SUB), :]

        for dx in range(-radius, radius + 1):
            acc = tap_products(pad_d, own, images, rows, cols, dx, radius)
            for k, dy in enumerate(range(-radius, radius + 1)):
                sums_ref[0, pl.ds(9 + 7 * (dy + 3) + dx + 3, 1), :] = jnp.sum(
                    acc[k], axis=0, keepdims=True
                )

    by_radius(step, radii, conv_back)

    def second_half(lead):
        at = pl.ds(pl.multiple_of(lead * cells, cells), cells)
        dvalue = dvalue_f[at, :].astype(BF16)
        grads[at, 2 * LANES :] = dvalue
        sums_ref[0, pl.ds(62, 1), :] += jnp.sum(dvalue.astype(F32), axis=0, keepdims=True)
        back = dot_rt(grads[at, :], wq_ref[0])

        @pl.when(step == 0)
        def _():
            dnorma_ref[at, :] = back

        @pl.when(step > 0)
        def _():
            dnorma_ref[at, :] = dnorma_ref[at, :] + back

    loop(images, second_half)
    wide = 3 * LANES
    dw_ref[0, :, :wide] = dot_lt(norma_ref[...], grads[...]).astype(BF16)
    dw_ref[0, :, wide:] = dot_lt(low[...], attended_ref[0]).astype(BF16)


def input_back_kernel(
    dims,
    shape_ref,
    x_ref,
    first_ref,
    dnorma_ref,
    dsecond_ref,
    small_ref,
    grad_ref,
    sums_ref,
    pad_d,
    x_f,
):
    images, rows, cols, channels = dims
    cells = rows * cols
    pad_d[...] = jnp.zeros_like(pad_d)
    gain = small_ref[pl.ds(59, 1), :]

    def norm(r, acc):
        lead = r // rows
        y = r % rows
        at = pl.ds(pl.multiple_of(r * cols, cols), cols)
        normed, rstd = norm_parts(first_ref[at, :])
        back = dnorma_ref[at, :]
        dfirst = dsecond_ref[at, :] + norm_back(back, normed, rstd, gain)
        pad_d[lead, y, pl.ds(SUB, cols), :] = dfirst
        kept = col_keep(shape_ref, lead, cols, channels) & (y < shape_ref[lead, 0])
        x_f[at, :] = jnp.where(kept, x_ref[at, :].astype(F32), 0.0)
        terms = (dfirst, back * normed, back)
        return tuple(
            a + jnp.sum(t.reshape(cols // SUB, SUB, channels), axis=0)
            for a, t in zip(acc, terms)
        )

    zero = jnp.zeros((SUB, channels), F32)
    acc = lax.fori_loop(0, images * rows, norm, (zero,) * 3)
    sums_ref[...] = jnp.zeros_like(sums_ref)
    for k, a in enumerate(acc):
        sums_ref[pl.ds(9 + k, 1), :] = jnp.sum(a, axis=0, keepdims=True)

    def conv(lead):
        x = lax.broadcasted_iota(jnp.int32, (SUB, LANES), 0)
        for lane in range(0, channels, LANES):
            lanes = pl.ds(lane, LANES)
            for col in range(0, cols, SUB):
                out = filtered(
                    pad_d,
                    lead,
                    rows,
                    col,
                    lambda dy, dx: small_ref[pl.ds(3 * (dy + 1) + dx + 1, 1), lanes],
                    1,
                    -1,
                    lanes,
                )
                inside = (x + col) < shape_ref[lead, 1]
                for y in range(rows):
                    own = pad_d[lead, y, pl.ds(SUB + col, SUB), lanes]
                    at = pl.multiple_of(lead * cells + (y * cols + col), SUB)
                    kept = inside & (y < shape_ref[lead, 0])
                    grad_ref[pl.ds(at, SUB), lanes] = jnp.where(kept, own + out[y], 0.0)

    loop(images, conv)
    for lane in range(0, channels, LANES):
        lanes = pl.ds(lane, LANES)

        def own(lead, y, col):
            at = pl.multiple_of(lead * cells + (y * cols + col), SUB)
            return x_f[pl.ds(at, SUB), lanes]

        for dx in (-1, 0, 1):
            acc = tap_products(pad_d, own, images, rows, cols, dx, 1, lanes)
            for k, dy in enumerate((-1, 0, 1)):
                sums_ref[pl.ds(3 * (dy + 1) + dx + 1, 1), lanes] = jnp.sum(
                    acc[k], axis=0, keepdims=True
                )


def whole(shape):
    return pl.BlockSpec(shape, lambda *_: (0,) * len(shape))


def part(shape):
    return pl.BlockSpec((1, *shape), lambda j: (j,) + (0,) * len(shape))


SCALARS = pl.BlockSpec(memory_space=pltpu.SMEM)
PARAMS = pltpu.CompilerParams(vmem_limit_bytes=VMEM_LIMIT)


def shape_of(shape, dtype):
    return jax.ShapeDtypeStruct(shape, dtype)


def attention(dims, radii, grids, x, small, parts, wq, wp):
    images, rows, cols, channels = dims
    cells = images * rows * cols
    groups = wq.shape[0]
    kinds = ((cells, LANES),) * 5 + ((images, LANES, LANES),)
    return pl.pallas_call(
        functools.partial(attention_kernel, dims, radii),
        grid=(groups,),
        in_specs=[
            SCALARS,
            whole((cells, channels)),
            whole(small.shape),
            part(parts.shape[1:]),
            part(wq.shape[1:]),
            part(wp.shape[1:]),
        ],
        out_specs=[
            whole((cells, channels)),
            whole((cells, channels)),
            *[part(k) for k in kinds],
            whole((cells, channels)),
            whole((cells, channels)),
        ],
        out_shape=[
            shape_of((cells, channels), F32),
            shape_of((cells, channels), BF16),
            *[shape_of((groups, *k), BF16) for k in kinds],
            shape_of((cells, channels), F32),
            shape_of((cells, channels), BF16),
        ],
        scratch_shapes=[
            pltpu.VMEM((images, rows, cols + 2 * SUB, channels), F32),
            pltpu.VMEM((images, rows, cols + 2 * SUB, LANES), F32),
            pltpu.VMEM((cells, LANES), F32),
            pltpu.VMEM((cells, channels), F32),
        ],
        compiler_params=PARAMS,
        name="attention",
    )(grids, x, small, parts, wq, wp)


def hidden_part(dims, grids, cot, normb, second, small, bias, w1, w2):
    images, rows, cols, channels = dims
    cells = images * rows * cols
    groups, _, hidden = w1.shape
    return pl.pallas_call(
        functools.partial(hidden_kernel, dims),
        grid=(groups,),
        in_specs=[
            SCALARS,
            whole((cells, channels)),
            whole((cells, channels)),
            whole((cells, channels)),
            whole(small.shape),
            part(bias.shape[1:]),
            part(w1.shape[1:]),
            part(w2.shape[1:]),
        ],
        out_specs=[
            whole((cells, channels)),
            whole((cells, channels)),
            part((channels, 2 * hidden)),
            part((1, hidden)),
            whole((SUB, channels)),
        ],
        out_shape=[
            shape_of((cells, channels), BF16),
            shape_of((cells, channels), F32),
            shape_of((groups, channels, 2 * hidden), BF16),
            shape_of((groups, 1, hidden), F32),
            shape_of((SUB, channels), F32),
        ],
        scratch_shapes=[
            pltpu.VMEM((cells, channels), BF16),
            pltpu.VMEM((rows * cols, hidden), F32),
            pltpu.VMEM((rows * cols, hidden), F32),
            pltpu.VMEM((cells, hidden), BF16),
            pltpu.VMEM((cells, hidden), BF16),
            pltpu.VMEM((cells, channels), F32),
            pltpu.VMEM((cells, channels), F32),
        ],
        compiler_params=PARAMS,
        name="hidden",
    )(grids, cot, normb, second, small, bias, w1, w2)


def attention_back(dims, radii, grids, dsecond, norma, parts, wq, wp, saved):
    images, rows, cols, channels = dims
    cells = images * rows * cols
    groups = wq.shape[0]
    return pl.pallas_call(
        functools.partial(attention_back_kernel, dims, radii),
        grid=(groups,),
        in_specs=[
            SCALARS,
            whole((cells, channels)),
            whole((cells, channels)),
            part(parts.shape[1:]),
            part(wq.shape[1:]),
            part(wp.shape[1:]),
            *[part(s.shape[1:]) for s in saved],
        ],
        out_specs=[
            whole((cells, channels)),
            part((channels, 4 * LANES)),
            part((72, LANES)),
        ],
        out_shape=[
            shape_of((cells, channels), F32),
            shape_of((groups, channels, 4 * LANES), BF16),
            shape_of((groups, 72, LANES), F32),
        ],
        scratch_shapes=[
            pltpu.VMEM((cells, channels), BF16),
            pltpu.VMEM((images, rows, cols + 2 * SUB, LANES), F32),
            pltpu.VMEM((cells, LANES), F32),
            pltpu.VMEM((cells, 3 * LANES), BF16),
            pltpu.VMEM((cells, LANES), F32),
        ],
        compiler_params=PARAMS,
        name="attention_back",
    )(grids, dsecond, norma, parts, wq, wp, *saved)


def input_back(dims, grids, x, first, dnorma, dsecond, small):
    images, rows, cols, channels = dims
    cells = images * rows * cols
    return pl.pallas_call(
        functools.partial(input_back_kernel, dims),
        grid=(1,),
        in_specs=[
            SCALARS,
            whole((cells, channels)),
            whole((cells, channels)),
            whole((cells, channels)),
            whole((cells, channels)),
            whole(small.shape),
        ],
        out_specs=[whole((cells, channels)), whole((16, channels))],
        out_shape=[shape_of((cells, channels), F32), shape_of((16, channels), F32)],
        scratch_shapes=[
            pltpu.VMEM((images, rows, cols + 2 * SUB, channels), F32),
            pltpu.VMEM((cells, channels), F32),
        ],
        compiler_params=PARAMS,
        name="input_back",
    )(grids, x, first, dnorma, dsecond, small)


def adamw(weight, mean, square, gradient, factor, rate, decay):
    clipped = gradient * factor
    mean_new = BETA_ONE * mean + (1.0 - BETA_ONE) * clipped
    square_new = BETA_TWO * square + (1.0 - BETA_TWO) * clipped * clipped
    mean_hat = mean_new / (1.0 - BETA_ONE**STEP)
    square_hat = square_new / (1.0 - BETA_TWO**STEP)
    weight_new = weight - rate * (mean_hat / (jnp.sqrt(square_hat) + ADAM_EPS) + decay * weight)
    return (weight_new, mean_new, square_new)


def window_rows(channels):
    radius = jnp.repeat(jnp.array([radius_of(h) for h in range(channels // HD)], jnp.int32), HD)
    tap_list = jnp.arange(49, dtype=jnp.int32)
    tap_row = jnp.abs(tap_list // 7 - 3)
    tap_col = jnp.abs(tap_list % 7 - 3)
    inside = (tap_row[:, None] <= radius[None, :]) & (tap_col[:, None] <= radius[None, :])
    return inside.astype(F32)


def on_device(
    patches,
    cotangent,
    grid_shape,
    qkv_weight,
    qkv_mean,
    qkv_square,
    proj_weight,
    proj_mean,
    proj_square,
    expand_weight,
    expand_mean,
    expand_square,
    contract_weight,
    contract_mean,
    contract_square,
    small_params,
    small_mean,
    small_square,
):
    group = lax.axis_size("mp")
    shards = lax.axis_size("dp")
    place = lax.axis_index("mp")
    local_rows, image_count, cols, channels = patches.shape
    images = image_count // group
    rows = local_rows * group
    dims = (images, rows, cols, channels)
    cells = images * rows * cols
    head_width = qkv_weight.shape[2]
    hidden = expand_weight.shape[1]
    assert head_width == LANES
    per_block = head_width // HD
    radii = [
        max(radius_of(per_block * g + h) for h in range(per_block)) for g in range(group)
    ]
    grids = lax.dynamic_slice_in_dim(grid_shape, place * images, images, 0)

    x = to_images(patches).reshape(cells, channels)

    def whole_weight(weight):
        rows_here = weight.shape[0]
        weight = weight.astype(BF16).reshape(rows_here, -1)
        every = gathered(gathered(weight, "dp").reshape(shards * rows_here, -1), "mp")
        return every

    wq = whole_weight(qkv_weight)
    wp = whole_weight(proj_weight)
    cot = to_images(cotangent.astype(BF16)).reshape(cells, channels)
    w1 = whole_weight(expand_weight)
    w2 = whole_weight(contract_weight)

    window = window_rows(channels)
    masked_small = jnp.concatenate(
        [small_params[:9], small_params[9:58] * window, small_params[58:]], axis=0
    )
    parts = masked_small.reshape(72, group, LANES).transpose(1, 0, 2)
    unit_bias = small_params[68:].reshape(group, 1, hidden)

    first, norma, *saved, second, normb = attention(
        dims, radii, grids, x, small_params, parts, wq, wp
    )
    out, dsecond, dw_hidden, dbias, sums_two = hidden_part(
        dims, grids, cot, normb, second, small_params, unit_bias, w1, w2
    )
    block_out = to_rows(out.reshape(dims))
    dnorma, dw_heads, sums_heads = attention_back(
        dims, radii, grids, dsecond, norma, parts, wq, wp, saved
    )
    grad, sums_one = input_back(dims, grids, x, first, dnorma, dsecond, small_params)
    patch_grad = to_rows(grad.astype(BF16).reshape(dims)).astype(F32)

    def own_share(grads):
        tiles = grads.reshape(group, shards, channels // shards, grads.shape[-1])
        return halved(halved(tiles, "mp", 0), "dp", 0).astype(F32)

    shard_hidden = own_share(dw_hidden)
    shard_heads = own_share(dw_heads)
    shard_expand = shard_hidden[:, :hidden]
    shard_contract = shard_hidden[:, hidden:]
    shard_qkv = shard_heads[:, : 3 * LANES].reshape(-1, 3, LANES)
    shard_proj = shard_heads[:, 3 * LANES :]

    heads_rows = sums_heads.transpose(1, 0, 2).reshape(72, channels)
    small_local = jnp.concatenate(
        [
            sums_one[:9],
            heads_rows[9:58] * window,
            sums_one[9:12],
            heads_rows[61:64],
            sums_two[:4],
            dbias.reshape(-1, channels),
        ],
        axis=0,
    )
    count = group * shards
    both = ("dp", "mp")
    tiles = lax.all_to_all(small_local.reshape(count, -1), both, 0, 0, tiled=True)
    own_small = jnp.sum(tiles, axis=0)
    local_sq = (
        jnp.sum(shard_heads * shard_heads)
        + jnp.sum(shard_hidden * shard_hidden)
        + jnp.sum(own_small * own_small)
    )
    message = jnp.concatenate([own_small, jnp.full((LANES,), local_sq, F32)])
    every = lax.all_to_all(
        jnp.broadcast_to(message, (count, message.shape[0])), both, 0, 0, tiled=True
    )
    grad_small = every[:, : own_small.shape[0]].reshape(small_params.shape)
    grad_norm = jnp.sqrt(jnp.sum(every[:, own_small.shape[0]]))
    factor = jnp.minimum(1.0, CLIP_NORM / (grad_norm + 1e-06))
    rate_model = RATE_FACTOR * D ** (-0.5)
    rate_hidden = RATE_FACTOR * FF ** (-0.5)
    qkv_new = adamw(qkv_weight, qkv_mean, qkv_square, shard_qkv, factor, rate_model, WEIGHT_DECAY)
    proj_new = adamw(
        proj_weight, proj_mean, proj_square, shard_proj, factor, rate_model, WEIGHT_DECAY
    )
    expand_new = adamw(
        expand_weight, expand_mean, expand_square, shard_expand, factor, rate_model, WEIGHT_DECAY
    )
    contract_new = adamw(
        contract_weight,
        contract_mean,
        contract_square,
        shard_contract,
        factor,
        rate_hidden,
        WEIGHT_DECAY,
    )
    small_new = adamw(small_params, small_mean, small_square, grad_small, factor, SMALL_RATE, 0.0)
    return (
        block_out,
        patch_grad,
        grad_norm,
        *qkv_new,
        *proj_new,
        *expand_new,
        *contract_new,
        *small_new,
    )


def solution(mesh):
    cells = P("mp", "dp", None, None)
    heads = P("dp", None, "mp")
    matrix = P("dp", "mp")
    params = [heads] * 3 + [matrix] * 9 + [P()] * 3
    return jax.shard_map(
        on_device,
        mesh=mesh,
        in_specs=(cells, cells, P("dp", None), *params),
        out_specs=(cells, cells, P(), *params),
        check_vma=False,
    )
```

time: 879 us -> 382 us (0.43)
  waiting for transfers between devices: 285 us -> 117 us
  blocking collectives: 160 us -> 0 us
  other arithmetic: 202 us -> 44.1 us
  Pallas kernels: 0 us -> 126 us
  matrix products: 86.9 us -> 0 us
  local copies, waits for them, and re-layouts: 106 us -> 24 us
  starting transfers between devices: 12.9 us -> 62.6 us
  between operations: 21.4 us -> 5.14 us
    pallas_call x0 -> x4, Pallas kernels: none -> 126 us  [the longest x1 39 us: hidden_part(): pl.pallas_call(functools.partial(hidden_kernel, dims), grid=(groups,), in...]
    all_gather x4 -> x0, blocking collectives: 120 us -> none  [the longest x1 31.7 us: on_device(): lax.all_gather(qkv_weight.astype(jnp.bfloat16), 'dp', axis=0, tiled=True)]
    psum x1 -> x0, waiting for transfers between devices: 119 us -> none  [on_device(): grad_small = lax.psum(small_local, ('dp', 'mp'))]
    reduce_scatter x4 -> x0, waiting for transfers between devices: 114 us -> none  [the longest x1 51.1 us: on_device(): lax.psum_scatter(jnp.einsum('yixe,de->yixd', piece, proj_all, preferred_e...]
    ppermute x4 -> x30, waiting for transfers between devices: 2.68 us -> 106 us  [flip(): return lax.ppermute(array, axis, [(i, i ^ 1 << bit) for i in range(size)])]
    reduce_sum x19 -> x5, other arithmetic: 100 us -> 2.62 us  [the longest x1 0.67 us: on_device(): jnp.sum(shard_hidden * shard_hidden)]
    dot_general x18 -> x0, matrix products: 86.9 us -> none  [the longest x1 8.85 us: on_device(): jnp.einsum('yixd,df->yixf', grad_all, contract_all, preferred_element_typ...]
    convert_element_type x14 -> x12, other arithmetic: 82 us -> 14.2 us  [the longest x8 11 us: halved(): array = (mine.astype(F32) + got.astype(F32)).astype(array.dtype)]
  transfers between devices with their start and end apart: 14 -> 36, of which waited for: 7 -> 13; matrix products, arithmetic and copies ran while one was open for 11% -> 15% of each run, Pallas kernels for 0% -> 23%
where the time goes in v1:
time: 382 us; the launch traced here: 379 us
  Pallas kernels  126 us (33%)
  waiting for transfers between devices  117 us (31%)
  starting transfers between devices  62.6 us (16%)
  other arithmetic  44.1 us (12%)
  local copies, waits for them, and re-layouts  24 us (6%)
  between operations  5.14 us (1%)
    ppermute x30, waiting for transfers between devices, flip(): return lax.ppermute(array, axis, [(i, i ^ 1 << bit) for i in range(size)])  106 us
    pallas_call x1, Pallas kernels, hidden_part(): pl.pallas_call(functools.partial(hidden_kernel, dims), grid=(groups,), in...  39 us
    pallas_call x1, Pallas kernels, attention(): pl.pallas_call(functools.partial(attention_kernel, dims, radii), grid=(gr...  36.6 us
    ppermute x30, starting transfers between devices, flip(): return lax.ppermute(array, axis, [(i, i ^ 1 << bit) for i in range(size)])  36.5 us
    pallas_call x1, Pallas kernels, attention_back(): pl.pallas_call(functools.partial(attention_back_kernel, dims, radii), gri...  31.2 us
    select_n x20, other arithmetic, gathered(): jnp.where(upper, jnp.concatenate([other, array], axis=0), jnp.concatenate...  21.7 us
    pallas_call x1, Pallas kernels, input_back(): pl.pallas_call(functools.partial(input_back_kernel, dims), grid=(1,), in_...  19 us
    convert_element_type x8, other arithmetic, halved(): array = (mine.astype(F32) + got.astype(F32)).astype(array.dtype)  11 us
  transfers between devices with their start and end apart: 36, of which 13 were waited for; matrix products, arithmetic and copies ran while one was open for 15% of the time, Pallas kernels for 23%

profile of v1, /device:TPU:8, one launch (start us, length us, event | category | flops | bytes accessed | tf_op | source)
XLA Modules:
  0.0 378.6 jit_solution(5768593920570047401)
XLA Ops:
  6.9 3.5 all-to-all-start.1
  17.5 4.1 %collective-permute-done.11 = bf16[2,64,512]{2,1,0:T(8,128)(2,1)S(1)} collective-permute-done((bf16[2,64,512]{2,1,0:T(8,128)(2,1)S(1)}, bf16[2,64,512]{2,1,0:T(8,128)(2,1)S(1)}, u32[]{:S(2)}, u32[]{:S(2)}) %collective-permute-start.11) | collective-permute-done | bytes 131104 | tf_op jit(solution)/shard_map/ppermute | solution.py:48
  24.3 4.1 %collective-permute-start.2 = (bf16[4,64,384]{2,1,0:T(8,128)(2,1)S(1)}, bf16[4,64,384]{2,1,0:T(8,128)(2,1)S(1)}, u32[]{:S(2)}, u32[]{:S(2)}) collective-permute-start(bf16[4,64,384]{2,1,0:T(8,128)(2,1)S(1)} %maximum_select_fusion.13), channel_id=1, source_target_pairs={{0,16},{4,20},{8,24},{12,28},{16,0},{20,4},{24,8},{28,12},{1,17},{... | collective-permute-start | bytes 589832 | tf_op jit(solution)/shard_map/ppermute | solution.py:48
  30.4 14.7 %collective-permute-done.12 = bf16[4,64,512]{2,1,0:T(8,128)(2,1)S(1)} collective-permute-done((bf16[4,64,512]{2,1,0:T(8,128)(2,1)S(1)}, bf16[4,64,512]{2,1,0:T(8,128)(2,1)S(1)}, u32[]{:S(2)}, u32[]{:S(2)}) %collective-permute-start.12) | collective-permute-done | bytes 262176 | tf_op jit(solution)/shard_map/ppermute | solution.py:48
  46.0 3.3 collective-permute-done.2
  53.5 3.4 collective-permute-start.7
  67.3 4.6 %all-to-all-start = ((bf16[4,4,2,32,512]{4,3,1,2,0:T(8,128)(2,1)}), bf16[4,4,2,32,512]{4,3,1,2,0:T(8,128)(2,1)}, u32[]{:S(2)}, u32[]{:S(2)}) async-start(bf16[4,4,2,32,512]{4,3,1,2,0:T(8,128)(2,1)} %bitcast.1), calls=%async_computation | async-start | bytes 2097152 | tf_op jit(solution)/shard_map/all_to_all | solution.py:86
  77.6 67.0 %collective-permute-done.9 = bf16[2,512,128]{2,1,0:T(8,128)(2,1)S(1)} collective-permute-done((bf16[2,512,128]{2,1,0:T(8,128)(2,1)S(1)}, bf16[2,512,128]{2,1,0:T(8,128)(2,1)S(1)}, u32[]{:S(2)}, u32[]{:S(2)}) %collective-permute-start.9) | collective-permute-done | bytes 262176 | tf_op jit(solution)/shard_map/ppermute | solution.py:48
  148.9 3.4 maximum_select_fusion.2.wq_ref
  152.3 36.6 %attention.1 = (f32[1024,512]{1,0:T(8,128)}, bf16[1024,512]{1,0:T(8,128)(2,1)}, bf16[4,1024,128]{2,1,0:T(8,128)(2,1)}, bf16[4,1024,128]{2,1,0:T(8,128)(2,1)}, bf...) custom-call(s32[2,2]{1,0:T(2,128)} %copy.104.shape_ref, ...), custom_call_target="tpu_custom_call" | custom-call | tf_op jit(solution)/shard_map/attention/pallas_call | solution.py:673
  188.9 3.3 maximum_select_fusion.w1_ref
  192.2 3.4 maximum_select_fusion.1.w2_ref
  195.6 39.0 %hidden.1 = (bf16[1024,512]{1,0:T(8,128)(2,1)}, f32[1024,512]{1,0:T(8,128)}, bf16[4,512,1024]{2,1,0:T(8,128)(2,1)}, f32[4,1,512]{2,1,0:T(1,128)}, f32[8,512]{1,0:T(8,128)}) custom-call(s32[2,2]{1,0:T(2,128)} %copy.104.shape_ref, bf16[1024,512]{1,0:T(8,128)(2,1)} %bitcast.134, bf16[1024,512]{1,0:T(8,128)(2,1)} %get-tuple-element.38.normb_ref, ...), custom_call_target="tpu_custom_call" | custom-call | tf_op jit(solution)/shard_map/hidden/pallas_call | solution.py:713
  236.6 31.2 %attention_back.1 = (f32[1024,512]{1,0:T(8,128)}, bf16[4,512,512]{2,1,0:T(8,128)(2,1)}, f32[4,72,128]{2,1,0:T(8,128)}) custom-call(s32[2,2]{1,0:T(2,128)} %copy.104.shape_ref, f32[1024,512]{1,0:T(8,128)} %get-tuple-element.42.dsecond_ref, bf16[1024,512]{1,0:T(8,128)(2,1)} %get-tuple-element.43.norma_ref, f32[4,72,128]{2,1,0:T(8,128)} %bitcast_bitcast_fusion.part_ref, ...), custom_call_target="tpu_custom_call" | custom-call | tf_op jit(solution)/shard_map/attention_back/pallas_call | solution.py:758
  269.7 3.3 fusion
  278.8 19.0 %input_back.1 = (f32[1024,512]{1,0:T(8,128)}, f32[16,512]{1,0:T(8,128)}) custom-call(s32[2,2]{1,0:T(2,128)} %copy.104.shape_ref, bf16[1024,512]{1,0:T(8,128)(2,1)} %bitcast.125, f32[1024,512]{1,0:T(8,128)} %get-tuple-element.41.first_ref, f32[1024,512]{1,0:T(8,128)} %get-tuple-element.50.dnorma_ref, f32[1024,512]{1,0:T(8,128)} %get-tuple-element.42.dsecond_ref, ...), custom_call_target="tpu_custom_call" | custom-call | tf_op jit(solution)/shard_map/input_back/pallas_call | solution.py:795
  300.5 5.7 %all-to-all-start.4 = ((f32[32,1,1152]{2,1,0:T(1,128)}), f32[32,1,1152]{2,1,0:T(1,128)S(1)}, u32[]{:S(2)}, u32[]{:S(2)}) async-start(f32[32,1,1152]{2,1,0:T(1,128)} %all_to_all.32), calls=%async_computation.4 | async-start | bytes 294912 | tf_op jit(solution)/shard_map/all_to_all | solution.py:932
  306.2 5.7 %collective-permute-done.21 = bf16[8,64,512]{2,1,0:T(8,128)(2,1)} collective-permute-done((bf16[8,64,512]{2,1,0:T(8,128)(2,1)}, bf16[8,64,512]{2,1,0:T(8,128)(2,1)}, u32[]{:S(2)}, u32[]{:S(2)}) %collective-permute-start.21) | collective-permute-done | bytes 524320 | tf_op jit(solution)/shard_map/ppermute | solution.py:48
  322.4 3.5 all-to-all-start.3
  336.8 3.6 all-to-all-done.3
  340.3 3.5 all-to-all-start.2
  348.5 4.8 %collective-permute-done.29 = bf16[64,1024]{1,0:T(8,128)(2,1)S(1)} collective-permute-done((bf16[64,1024]{1,0:T(8,128)(2,1)S(1)}, bf16[64,1024]{1,0:T(8,128)(2,1)S(1)}, u32[]{:S(2)}, u32[]{:S(2)}) %collective-permute-start.29) | collective-permute-done | bytes 131104 | tf_op jit(solution)/shard_map/ppermute | solution.py:48
  359.1 5.3 %all-to-all-start.5 = ((f32[32,1,1280]{2,1,0:T(1,128)}), f32[32,1,1280]{2,1,0:T(1,128)S(1)}, u32[]{:S(2)}, u32[]{:S(2)}) async-start(f32[32,1,1280]{2,1,0:T(1,128)} %broadcast_in_dim.22), calls=%async_computation.5 | async-start | bytes 327680 | tf_op jit(solution)/shard_map/all_to_all | solution.py:940
  367.4 4.6 %all-to-all-done.5 = f32[32,1,1280]{2,1,0:T(1,128)S(1)} async-done(((f32[32,1,1280]{2,1,0:T(1,128)}), f32[32,1,1280]{2,1,0:T(1,128)S(1)}, u32[]{:S(2)}, u32[]{:S(2)}) %all-to-all-start.5) | async-done | bytes 163872 | tf_op jit(solution)/shard_map/all_to_all | solution.py:940
  (204 shorter events, 92.7 us)
Async XLA Ops:
  1.7 13.6 %collective-permute-start = (bf16[1,64,384]{2,1,0:T(8,128)(2,1)S(1)}, bf16[1,64,384]{2,1,0:T(8,128)(2,1)S(1)}, u32[]{:S(2)}, u32[]{:S(2)}) collective-permute-start(bf16[1,64,384]{2,1,0:T(8,128)(2,1)S(1)} %broadcast_in_dim_reshape.2), channel_id=1, source_target_pairs={{0,4},{4,0},{8,12},{12,8},{16,20},{20,16},{24,28},{28,24},{1,5},{5... | collective-permute-start | bytes 147464 | tf_op jit(solution)/shard_map/ppermute | solution.py:48
  4.0 26.2 %collective-permute-start.5 = (bf16[1,64,128]{2,1,0:T(8,128)(2,1)S(1)}, bf16[1,64,128]{2,1,0:T(8,128)(2,1)S(1)}, u32[]{:S(2)}, u32[]{:S(2)}) collective-permute-start(bf16[1,64,128]{2,1,0:T(8,128)(2,1)S(1)} %convert_bitcast_fusion.2), channel_id=1, source_target_pairs={{0,4},{4,0},{8,12},{12,8},{16,20},{20,16},{24,28},{28,24},{1,5},{5... | collective-permute-start | bytes 49160 | tf_op jit(solution)/shard_map/ppermute | solution.py:48
  6.9 60.4 %all-to-all-start.1 = ((bf16[4,4,2,32,512]{4,3,1,2,0:T(8,128)(2,1)}), bf16[4,4,2,32,512]{4,3,1,2,0:T(8,128)(2,1)S(1)}, u32[]{:S(2)}, u32[]{:S(2)}) async-start(bf16[4,4,2,32,512]{4,3,1,2,0:T(8,128)(2,1)} %bitcast.5), calls=%async_computation.1 | async-start | bytes 2097152 | tf_op jit(solution)/shard_map/all_to_all | solution.py:86
  21.7 23.5 %collective-permute-start.12 = (bf16[4,64,512]{2,1,0:T(8,128)(2,1)S(1)}, bf16[4,64,512]{2,1,0:T(8,128)(2,1)S(1)}, u32[]{:S(2)}, u32[]{:S(2)}) collective-permute-start(bf16[4,64,512]{2,1,0:T(8,128)(2,1)S(1)} %maximum_select_fusion.11), channel_id=1, source_target_pairs={{0,16},{4,20},{8,24},{12,28},{16,0},{20,4},{24,8},{28,12},{1,17},{... | collective-permute-start | bytes 786440 | tf_op jit(solution)/shard_map/ppermute | solution.py:48
  24.3 25.0 %collective-permute-start.2 = (bf16[4,64,384]{2,1,0:T(8,128)(2,1)S(1)}, bf16[4,64,384]{2,1,0:T(8,128)(2,1)S(1)}, u32[]{:S(2)}, u32[]{:S(2)}) collective-permute-start(bf16[4,64,384]{2,1,0:T(8,128)(2,1)S(1)} %maximum_select_fusion.13), channel_id=1, source_target_pairs={{0,16},{4,20},{8,24},{12,28},{16,0},{20,4},{24,8},{28,12},{1,17},{... | collective-permute-start | bytes 589832 | tf_op jit(solution)/shard_map/ppermute | solution.py:48
  28.5 24.1 %collective-permute-start.17 = (bf16[4,64,512]{2,1,0:T(8,128)(2,1)S(1)}, bf16[4,64,512]{2,1,0:T(8,128)(2,1)S(1)}, u32[]{:S(2)}, u32[]{:S(2)}) collective-permute-start(bf16[4,64,512]{2,1,0:T(8,128)(2,1)S(1)} %maximum_select_fusion.12), channel_id=1, source_target_pairs={{0,16},{4,20},{8,24},{12,28},{16,0},{20,4},{24,8},{28,12},{1,17},{... | collective-permute-start | bytes 786440 | tf_op jit(solution)/shard_map/ppermute | solution.py:48
  30.2 23.3 %collective-permute-start.6 = (bf16[2,64,128]{2,1,0:T(8,128)(2,1)S(1)}, bf16[2,64,128]{2,1,0:T(8,128)(2,1)S(1)}, u32[]{:S(2)}, u32[]{:S(2)}) collective-permute-start(bf16[2,64,128]{2,1,0:T(8,128)(2,1)S(1)} %maximum_select_fusion.19), channel_id=1, source_target_pairs={{0,8},{4,12},{8,0},{12,4},{16,24},{20,28},{24,16},{28,20},{1,9},{5... | collective-permute-start | bytes 98312 | tf_op jit(solution)/shard_map/ppermute | solution.py:48
  46.0 14.9 %collective-permute-start.13 = (bf16[1,512,512]{2,1,0:T(8,128)(2,1)}, bf16[1,512,512]{2,1,0:T(8,128)(2,1)}, u32[]{:S(2)}, u32[]{:S(2)}) collective-permute-start(bf16[1,512,512]{2,1,0:T(8,128)(2,1)} %bitcast.13), channel_id=1, source_target_pairs={{0,1},{1,0},{2,3},{3,2},{4,5},{5,4},{6,7},{7,6},{8,9},{9,8},{10,11... | collective-permute-start | bytes 1572872 | tf_op jit(solution)/shard_map/ppermute | solution.py:48
  50.1 14.1 %collective-permute-start.3 = (bf16[1,512,384]{2,1,0:T(8,128)(2,1)}, bf16[1,512,384]{2,1,0:T(8,128)(2,1)}, u32[]{:S(2)}, u32[]{:S(2)}) collective-permute-start(bf16[1,512,384]{2,1,0:T(8,128)(2,1)} %bitcast.9), channel_id=1, source_target_pairs={{0,1},{1,0},{2,3},{3,2},{4,5},{5,4},{6,7},{7,6},{8,9},{9,8},{10,11... | collective-permute-start | bytes 1179656 | tf_op jit(solution)/shard_map/ppermute | solution.py:48
  53.5 18.4 %collective-permute-start.18 = (bf16[1,512,512]{2,1,0:T(8,128)(2,1)}, bf16[1,512,512]{2,1,0:T(8,128)(2,1)}, u32[]{:S(2)}, u32[]{:S(2)}) collective-permute-start(bf16[1,512,512]{2,1,0:T(8,128)(2,1)} %bitcast.15), channel_id=1, source_target_pairs={{0,1},{1,0},{2,3},{3,2},{4,5},{5,4},{6,7},{7,6},{8,9},{9,8},{10,11... | collective-permute-start | bytes 1572872 | tf_op jit(solution)/shard_map/ppermute | solution.py:48
  60.8 14.6 %collective-permute-start.8 = (bf16[1,512,128]{2,1,0:T(8,128)(2,1)S(1)}, bf16[1,512,128]{2,1,0:T(8,128)(2,1)}, u32[]{:S(2)}, u32[]{:S(2)}) collective-permute-start(bf16[1,512,128]{2,1,0:T(8,128)(2,1)S(1)} %bitcast.142), channel_id=1, source_target_pairs={{0,1},{1,0},{2,3},{3,2},{4,5},{5,4},{6,7},{7,6},{8,9},{9,8},{10,11... | collective-permute-start | bytes 393224 | tf_op jit(solution)/shard_map/ppermute | solution.py:48
  62.8 126.1 %collective-permute-start.14 = (bf16[2,512,512]{2,1,0:T(8,128)(2,1)S(1)}, bf16[2,512,512]{2,1,0:T(8,128)(2,1)}, u32[]{:S(2)}, u32[]{:S(2)}) collective-permute-start(bf16[2,512,512]{2,1,0:T(8,128)(2,1)S(1)} %maximum_select_fusion.3), channel_id=1, source_target_pairs={{0,2},{1,3},{2,0},{3,1},{4,6},{5,7},{6,4},{7,5},{8,10},{9,11},{10,... | collective-permute-start | bytes 3145736 | tf_op jit(solution)/shard_map/ppermute | solution.py:48
  66.7 82.2 %collective-permute-start.4 = (bf16[2,512,384]{2,1,0:T(8,128)(2,1)}, bf16[2,512,384]{2,1,0:T(8,128)(2,1)}, u32[]{:S(2)}, u32[]{:S(2)}) collective-permute-start(bf16[2,512,384]{2,1,0:T(8,128)(2,1)} %maximum_select_fusion.5), channel_id=1, source_target_pairs={{0,2},{1,3},{2,0},{3,1},{4,6},{5,7},{6,4},{7,5},{8,10},{9,11},{10,... | collective-permute-start | bytes 2359304 | tf_op jit(solution)/shard_map/ppermute | solution.py:48
  67.3 79.3 %all-to-all-start = ((bf16[4,4,2,32,512]{4,3,1,2,0:T(8,128)(2,1)}), bf16[4,4,2,32,512]{4,3,1,2,0:T(8,128)(2,1)}, u32[]{:S(2)}, u32[]{:S(2)}) async-start(bf16[4,4,2,32,512]{4,3,1,2,0:T(8,128)(2,1)} %bitcast.1), calls=%async_computation | async-start | bytes 2097152 | tf_op jit(solution)/shard_map/all_to_all | solution.py:86
  73.6 118.6 %collective-permute-start.19 = (bf16[2,512,512]{2,1,0:T(8,128)(2,1)S(1)}, bf16[2,512,512]{2,1,0:T(8,128)(2,1)}, u32[]{:S(2)}, u32[]{:S(2)}) collective-permute-start(bf16[2,512,512]{2,1,0:T(8,128)(2,1)S(1)} %maximum_select_fusion.4), channel_id=1, source_target_pairs={{0,2},{1,3},{2,0},{3,1},{4,6},{5,7},{6,4},{7,5},{8,10},{9,11},{10,... | collective-permute-start | bytes 3145736 | tf_op jit(solution)/shard_map/ppermute | solution.py:48
  76.5 68.1 %collective-permute-start.9 = (bf16[2,512,128]{2,1,0:T(8,128)(2,1)S(1)}, bf16[2,512,128]{2,1,0:T(8,128)(2,1)S(1)}, u32[]{:S(2)}, u32[]{:S(2)}) collective-permute-start(bf16[2,512,128]{2,1,0:T(8,128)(2,1)S(1)} %maximum_select_fusion.10), channel_id=1, source_target_pairs={{0,2},{1,3},{2,0},{3,1},{4,6},{5,7},{6,4},{7,5},{8,10},{9,11},{10,... | collective-permute-start | bytes 786440 | tf_op jit(solution)/shard_map/ppermute | solution.py:48
  236.5 33.2 %collective-permute-start.25 = (bf16[2,8,64,1024]{3,2,1,0:T(8,128)(2,1)S(1)}, bf16[2,8,64,1024]{3,2,1,0:T(8,128)(2,1)}, u32[]{:S(2)}, u32[]{:S(2)}) collective-permute-start(bf16[2,8,64,1024]{3,2,1,0:T(8,128)(2,1)S(1)} %dynamic-slice_bitcast_fusion), channel_id=1, source_target_pairs={{0,1},{1,0},{2,3},{3,2},{4,5},{5,4},{6,7},{7,6},{8,9},{9,8},{10,11... | collective-permute-start | bytes 6291464 | tf_op jit(solution)/shard_map/ppermute | solution.py:48
  274.1 41.5 %collective-permute-start.26 = (bf16[8,64,1024]{2,1,0:T(8,128)(2,1)}, bf16[8,64,1024]{2,1,0:T(8,128)(2,1)}, u32[]{:S(2)}, u32[]{:S(2)}) collective-permute-start(bf16[8,64,1024]{2,1,0:T(8,128)(2,1)} %dynamic-slice_bitcast_fusion.1), channel_id=1, source_target_pairs={{0,2},{1,3},{2,0},{3,1},{4,6},{5,7},{6,4},{7,5},{8,10},{9,11},{10,... | collective-permute-start | bytes 3145736 | tf_op jit(solution)/shard_map/ppermute | solution.py:48
  277.9 34.0 %collective-permute-start.21 = (bf16[8,64,512]{2,1,0:T(8,128)(2,1)}, bf16[8,64,512]{2,1,0:T(8,128)(2,1)}, u32[]{:S(2)}, u32[]{:S(2)}) collective-permute-start(bf16[8,64,512]{2,1,0:T(8,128)(2,1)} %dynamic-slice_bitcast_fusion.4), channel_id=1, source_target_pairs={{0,2},{1,3},{2,0},{3,1},{4,6},{5,7},{6,4},{7,5},{8,10},{9,11},{10,... | collective-permute-start | bytes 1572872 | tf_op jit(solution)/shard_map/ppermute | solution.py:48
  300.5 21.9 %all-to-all-start.4 = ((f32[32,1,1152]{2,1,0:T(1,128)}), f32[32,1,1152]{2,1,0:T(1,128)S(1)}, u32[]{:S(2)}, u32[]{:S(2)}) async-start(f32[32,1,1152]{2,1,0:T(1,128)} %all_to_all.32), calls=%async_computation.4 | async-start | bytes 294912 | tf_op jit(solution)/shard_map/all_to_all | solution.py:932
  318.0 14.1 %collective-permute-start.27 = (bf16[2,2,64,1024]{3,2,1,0:T(8,128)(2,1)}, bf16[2,2,64,1024]{3,2,1,0:T(8,128)(2,1)}, u32[]{:S(2)}, u32[]{:S(2)}) collective-permute-start(bf16[2,2,64,1024]{3,2,1,0:T(8,128)(2,1)} %dynamic-slice_bitcast_fusion.3), channel_id=1, source_target_pairs={{0,4},{4,0},{8,12},{12,8},{16,20},{20,16},{24,28},{28,24},{1,5},{5... | collective-permute-start | bytes 1572872 | tf_op jit(solution)/shard_map/ppermute | solution.py:48
  322.4 18.0 %all-to-all-start.3 = ((bf16[4,2,4,32,512]{4,3,2,1,0:T(8,128)(2,1)}), bf16[4,2,4,32,512]{4,3,2,1,0:T(8,128)(2,1)S(1)}, u32[]{:S(2)}, u32[]{:S(2)}) async-start(bf16[4,2,4,32,512]{4,3,2,1,0:T(8,128)(2,1)} %bitcast.119), calls=%async_computation.3 | async-start | bytes 2097152 | tf_op jit(solution)/shard_map/all_to_all | solution.py:94
  340.3 18.0 %all-to-all-start.2 = ((bf16[4,2,4,32,512]{4,3,2,1,0:T(8,128)(2,1)}), bf16[4,2,4,32,512]{4,3,2,1,0:T(8,128)(2,1)S(1)}, u32[]{:S(2)}, u32[]{:S(2)}) async-start(bf16[4,2,4,32,512]{4,3,2,1,0:T(8,128)(2,1)} %bitcast.120), calls=%async_computation.2 | async-start | bytes 2097152 | tf_op jit(solution)/shard_map/all_to_all | solution.py:94
  359.1 12.9 %all-to-all-start.5 = ((f32[32,1,1280]{2,1,0:T(1,128)}), f32[32,1,1280]{2,1,0:T(1,128)S(1)}, u32[]{:S(2)}, u32[]{:S(2)}) async-start(f32[32,1,1280]{2,1,0:T(1,128)} %broadcast_in_dim.22), calls=%async_computation.5 | async-start | bytes 327680 | tf_op jit(solution)/shard_map/all_to_all | solution.py:940
  (43 other events, 484.2 us)
